TPU v7x, 32 devices: a whole 2x2x4 slice. The times are simulated.
32 devices in a mesh: ctx: 8 (over z, y), head: 4 (over x, core).
Axes of the slice: x: 2, y: 2, z: 4, core: 2. Of those that a mesh axis runs over, the one named last changes fastest.
Arguments:
- hidden: bfloat16 [2048, 2560], P('ctx'), may hold values from -6 to 6
- norm_gain: float32 [2560], replicated, may hold values from 0.1 to 1.9
- x_weight: bfloat16 [2560, 5120], P(None, 'head'), may hold values from -0.125 to 0.125
- z_weight: bfloat16 [2560, 5120], P(None, 'head'), may hold values from -0.125 to 0.125
- bc_weight: bfloat16 [2560, 256], replicated, may hold values from -0.125 to 0.125
- dt_weight: bfloat16 [2560, 80], P(None, 'head'), may hold values from -0.125 to 0.125
- x_kernel: float32 [4, 5120], P(None, 'head'), may hold values from -3 to 3
- bc_kernel: float32 [4, 256], replicated, may hold values from -3 to 3
- dt_bias: float32 [80], P('head'), may hold values from -1 to 1
- log_rate: float32 [80], P('head'), may hold values from -13 to -3
- out_gain: float32 [5120], P('head'), may hold values from 0.1 to 1.9
- out_weight: bfloat16 [5120, 2560], P('head'), may hold values from -0.078125 to 0.078125
Outputs:
- layer_out: bfloat16 [2048, 2560], P('ctx', 'head')
All inputs are finite; a program needn't handle non-finite values.
Results may differ from a plain program's by a relative error of at most 0.014.
Values may be sent and summed in bfloat16 or wider, within the bound.
A program may use at most 128 MiB of HBM per device.

v0:
```python
import jax
import jax.numpy as jnp
from jax import lax
from jax.sharding import PartitionSpec as P

HEAD_DIM = 64
STATE = 128


epsilon = 1e-05
highest = lax.Precision.HIGHEST


def from_behind(value, axis, steps):
    count = lax.axis_size(axis)
    first, last = (max(0, -steps), min(count, count - steps))
    return lax.ppermute(value, axis, [(source, source + steps) for source in range(first, last)])


def prefix(value, axis, join, neutral, backward):
    count = lax.axis_size(axis)
    place = lax.axis_index(axis)
    ahead = count - 1 - place if backward else place
    gathered = jax.tree.map(
        lambda a, kind: lax.all_gather(a.astype(kind), axis), value, (jnp.bfloat16, jnp.bfloat16)
    )
    state = jax.tree.map(lambda a, e: jnp.zeros_like(a) + jnp.asarray(e, a.dtype), value, neutral)

    def one(lap, state):
        source = count - 1 - lap if backward else lap
        return join(
            state,
            jax.tree.map(
                lambda a, own: lax.dynamic_index_in_dim(a, source, 0, False).astype(own.dtype),
                gathered,
                value,
            ),
        )

    return lax.fori_loop(0, ahead, one, state)


def rms_scale(values, scaling):
    mean_sq = jnp.mean(values * values, axis=-1, keepdims=True)
    return values * lax.rsqrt(mean_sq + epsilon) * scaling


def rim_prior(rim_rows):
    return from_behind(rim_rows, "ctx", 1)


def rim_next(rim_rows):
    return from_behind(rim_rows, "ctx", -1)


def link_states(earlier, later_part):
    return (earlier[0] * later_part[0], later_part[0][..., None, None] * earlier[1] + later_part[1])


def carry_prior(decays, states):
    identity = (jnp.ones_like(decays), jnp.zeros_like(states))
    return prefix((decays, states), "ctx", link_states, identity, False)[1]


def carry_next(decays, states):
    identity = (jnp.ones_like(decays), jnp.zeros_like(states))
    return prefix((decays, states), "ctx", link_states, identity, True)[1]


def conv_silu(extended, kernel, row_count):
    running = jnp.zeros(extended.shape[:1] + (row_count,) + extended.shape[2:], jnp.float32)
    for offset in range(kernel.shape[0]):
        running = running + kernel[offset] * extended[:, offset : offset + row_count].astype(
            jnp.float32
        )
    return jax.nn.silu(running).astype(jnp.bfloat16)


def mixer(stacked, params, fetch_rim, fetch_carry):
    (
        norm_gain,
        x_weight,
        z_weight,
        bc_weight,
        dt_weight,
        x_kernel,
        bc_kernel,
        dt_bias,
        log_rate,
        out_gain,
    ) = params
    count_dirs, row_count, model_width = stacked.shape
    normed = rms_scale(stacked.astype(jnp.float32), norm_gain).astype(jnp.bfloat16)
    normed = normed.reshape(count_dirs * row_count, model_width)
    x_in = jnp.dot(normed, x_weight, preferred_element_type=jnp.float32).astype(jnp.bfloat16)
    z_in = jnp.dot(normed, z_weight, preferred_element_type=jnp.float32).astype(jnp.bfloat16)
    bc_in = jnp.dot(normed, bc_weight, preferred_element_type=jnp.float32).astype(jnp.bfloat16)
    dt_raw = jnp.dot(normed, dt_weight, preferred_element_type=jnp.float32).reshape(
        count_dirs, row_count, -1
    )
    inner_width = x_in.shape[1]
    joined = jnp.concatenate([x_in, bc_in], axis=1).reshape(count_dirs, row_count, -1)
    tap_count = x_kernel.shape[0]
    rim_rows = fetch_rim(joined[:, row_count - tap_count + 1 :])
    extended = jnp.concatenate([rim_rows, joined], axis=1)
    kernel = jnp.concatenate([x_kernel, bc_kernel], axis=1)
    conv_out = conv_silu(extended, kernel, row_count)
    x_conv = conv_out[..., :inner_width]
    b_mat = conv_out[..., inner_width : inner_width + STATE]
    c_mat = conv_out[..., inner_width + STATE :]
    head_count = inner_width // HEAD_DIM
    step_size = jax.nn.softplus(dt_raw + dt_bias)
    log_decay = -step_size * jnp.exp(log_rate)
    cumulative = jnp.cumsum(log_decay, axis=1)
    cumul_heads = jnp.swapaxes(cumulative, 1, 2)
    step_heads = jnp.swapaxes(step_size, 1, 2)
    gram_rows = jnp.einsum("btn,bsn->bts", c_mat, b_mat, preferred_element_type=jnp.float32)
    causal = jnp.arange(row_count)[:, None] >= jnp.arange(row_count)[None, :]
    segment = cumul_heads[:, :, :, None] - cumul_heads[:, :, None, :]
    weights = (
        jnp.exp(jnp.where(causal, segment, -jnp.inf))
        * gram_rows[:, None]
        * step_heads[:, :, None, :]
    )
    x_float = x_conv.astype(jnp.float32).reshape(count_dirs, row_count, head_count, HEAD_DIM)
    b_float = b_mat.astype(jnp.float32)
    c_float = c_mat.astype(jnp.float32)
    within = jnp.einsum("bhts,bshp->bthp", weights, x_float, precision=highest)
    final_log = cumul_heads[:, :, -1]
    weight_end = jnp.exp(final_log[:, :, None] - cumul_heads) * step_heads
    local_state = jnp.einsum("bhs,bshp,bsn->bhpn", weight_end, x_float, b_float, precision=highest)
    carried = fetch_carry(jnp.exp(final_log), local_state)
    from_carry = (
        jnp.einsum("btn,bhpn->bthp", c_float, carried, precision=highest)
        * jnp.exp(cumulative)[..., None]
    )
    y_full = within + from_carry
    gating = jax.nn.silu(z_in.astype(jnp.float32)).reshape(
        count_dirs, row_count, head_count, HEAD_DIM
    )
    gated_out = rms_scale(y_full * gating, out_gain.reshape(head_count, HEAD_DIM))
    return gated_out.astype(jnp.bfloat16).reshape(count_dirs, row_count, inner_width)


def per_device(
    hidden,
    norm_gain,
    x_weight,
    z_weight,
    bc_weight,
    dt_weight,
    x_kernel,
    bc_kernel,
    dt_bias,
    log_rate,
    out_gain,
    out_weight,
):
    params = (
        norm_gain,
        x_weight,
        z_weight,
        bc_weight,
        dt_weight,
        x_kernel,
        bc_kernel,
        dt_bias,
        log_rate,
        out_gain,
    )
    forward_out = mixer(hidden[None], params, rim_prior, carry_prior)[0]
    backward_out = mixer(hidden[::-1, ::-1][None], params, rim_next, carry_next)[0][::-1]
    row_count = forward_out.shape[0]
    projected = jnp.dot(
        jnp.concatenate([forward_out, backward_out], axis=0),
        out_weight,
        preferred_element_type=jnp.float32,
    )
    partial_sum = projected[:row_count] + projected[row_count:, ::-1]
    summed = lax.psum_scatter(
        partial_sum.astype(jnp.bfloat16), "head", scatter_dimension=1, tiled=True
    ).astype(jnp.float32)
    first_col = lax.axis_index("head") * summed.shape[1]
    residual = lax.dynamic_slice_in_dim(hidden, first_col, summed.shape[1], 1).astype(jnp.float32)
    return (residual + summed).astype(jnp.bfloat16)


def solution(mesh):
    return jax.shard_map(
        per_device,
        mesh=mesh,
        in_specs=(
            P("ctx", None),
            P(),
            P(None, "head"),
            P(None, "head"),
            P(),
            P(None, "head"),
            P(None, "head"),
            P(),
            P("head"),
            P("head"),
            P("head"),
            P("head", None),
        ),
        out_specs=P("ctx", "head"),
        check_vma=False,
    )
```

profile of v0, /device:TPU:0, one launch (start us, length us, event | category | flops | bytes accessed | tf_op | source)
XLA Modules:
  0.0 265.9 jit_solution(13883786817986319440)
XLA Ops:
  6.5 1.8 fusion.12
  8.3 2.0 convolution_convert_fusion.5
  10.4 4.8 %convolution_convert_fusion.3 = bf16[256,1280]{1,0:T(8,128)(2,1)S(1)} fusion(bf16[2560,1280]{1,0:T(8,128)(2,1)} %param.18, bf16[256,2560]{1,0:T(8,128)(2,1)S(1)} %copy-done.2, f32[2560]{0:T(1024)S(1)} %copy-done.39, f32[256]{0:T(256)S(1)} %add_rsqrt_fusion.3), kind=kOutput, calls=%fused_computation.45 | convolution fusion | flops 1680670720 | bytes 8530944 | tf_op jit(solution)/shard_map/dot_general | solution.py:95
  16.2 4.9 %collective-permute-start = (bf16[1,3,1536]{2,1,0:T(4,128)(2,1)S(1)}, bf16[1,3,1536]{2,1,0:T(4,128)(2,1)S(1)}, u32[]{:S(2)}, u32[]{:S(2)}) collective-permute-start(bf16[1,3,1536]{2,1,0:T(4,128)(2,1)S(1)} %slice.109), channel_id=1, source_target_pairs={{0,4},{4,8},{8,12},{12,16},{16,20},{20,24},{24,28},{1,5},{5,9},{9,... | collective-permute-start | bytes 27656 | tf_op jit(solution)/shard_map/ppermute | solution.py:17
  21.1 14.4 %rev.9 = bf16[256,2560]{1,0:T(8,128)(2,1)} reverse(bf16[256,2560]{1,0:T(8,128)(2,1)S(1)} %copy-done.2), dimensions={0,1} | reverse | bytes 2621440 | tf_op jit(solution)/shard_map/rev | solution.py:172
  35.5 1.7 fusion.15
  37.2 2.0 convolution_convert_fusion.4
  39.2 4.8 %convolution_convert_fusion.1 = bf16[256,1280]{1,0:T(8,128)(2,1)S(1)} fusion(bf16[2560,1280]{1,0:T(8,128)(2,1)} %param.18, bf16[256,2560]{1,0:T(8,128)(2,1)S(1)} %copy-done.3, f32[256]{0:T(256)S(1)} %add_rsqrt_fusion.2, f32[2560]{0:T(1024)S(1)} %copy-done.39), kind=kOutput, calls=%fused_computation.42 | convolution fusion | flops 1680670720 | bytes 8530944 | tf_op jit(solution)/shard_map/dot_general | solution.py:95
  44.1 1.4 collective-permute-start.1
  46.3 1.3 negate_multiply_fusion.1
  50.9 5.6 %multiply_convert_fusion.1 = (bf16[1,256,1536]{2,1,0:T(8,128)(2,1)S(1)}, bf16[1,256,1536]{2,1,0:T(8,128)(2,1)S(1)}) fusion(bf16[1,3,1536]{2,1,0:T(4,128)(2,1)S(1)} %collective-permute-done, bf16[1,256,1536]{2,1,0:T(8,128)(2,1)} %copy-done.6, bf16[1,256,256]{2,1,0:T(8,128)(2,1)S(1)} %bitcast.196, bf16[1,256,1280]{2,1,0:T(8,128)(2,1)} %bitcast.184, ...), kind=kLoop, calls=%fused_computation.47 | loop fusion | flops 22020096 | bytes 4761600 | tf_op jit(solution)/shard_map/convert_element_type | solution.py:76
  57.5 2.3 copy.74
  59.8 2.6 fusion.63
  65.8 1.1 copy.90
  66.8 2.7 %fusion.66 = bf16[20,64,128]{2,1,0:T(8,128)(2,1)} fusion(bf16[256,20,64]{0,2,1:T(8,128)(2,1)} %bitcast.189, f32[256,20]{0,1:T(8,128)} %copy.100, bf16[1,256,1536]{2,1,0:T(8,128)(2,1)S(1)} %get-tuple-element.208), kind=kOutput, calls=%fused_computation.75 | convolution fusion | flops 504135680 | bytes 1069056 | tf_op jit(solution)/shard_map/bhs,bshp,bsn->bhpn/dot_general | solution.py:131
  71.2 1.4 copy.125
  72.5 1.4 copy.126
  74.7 1.6 copy.96
  81.8 1.6 copy.80
  83.4 1.6 copy.103
  85.7 6.0 %divide_multiply_fusion = f32[256,1280]{1,0:T(8,128)} fusion(bf16[2560,1280]{1,0:T(8,128)(2,1)} %param.19, bf16[256,2560]{1,0:T(8,128)(2,1)S(1)} %copy-done.4, f32[256]{0:T(256)} %copy-done.35, f32[2560]{0:T(1024)} %param.17), kind=kOutput, calls=%fused_computation.64 | convolution fusion | flops 1682309120 | bytes 9186304 | tf_op jit(solution)/shard_map/dot_general | solution.py:96
  91.7 2.8 %copy.104 = f32[256,1280]{0,1:T(8,128)} copy(f32[256,1280]{1,0:T(8,128)} %divide_multiply_fusion) | data formatting | bytes 2621440 | tf_op jit(solution)/shard_map/jit(silu)/mul | solution.py:138
  94.5 4.8 %divide_multiply_fusion.1 = f32[256,1280]{1,0:T(8,128)S(1)} fusion(bf16[2560,1280]{1,0:T(8,128)(2,1)} %param.19, bf16[256,2560]{1,0:T(8,128)(2,1)S(1)} %copy-done.2, f32[2560]{0:T(1024)S(1)} %copy-done.40, f32[256]{0:T(256)S(1)} %copy-done.34), kind=kOutput, calls=%fused_computation.70 | convolution fusion | flops 1682309120 | bytes 9186304 | tf_op jit(solution)/shard_map/dot_general | solution.py:96
  99.4 1.5 copy.88
  101.0 21.9 %all-gather.2 = bf16[8,20,1]{1,2,0:T(2,128)(2,1)S(1)} all-gather(bf16[1,20,1]{1,2,0:T(2,128)(2,1)S(1)} %copy-done.37), channel_id=4, replica_groups=mesh['ctx'=8,'head'=4] {'ctx'}, dimensions={0}, use_global_device_ids=true | all-gather | bytes 360 | tf_op jit(solution)/shard_map/all_gather | solution.py:25
  122.9 16.2 %all-gather = bf16[8,20,1]{1,2,0:T(2,128)(2,1)S(1)} all-gather(bf16[1,20,1]{1,2,0:T(2,128)(2,1)S(1)} %copy-done.36), channel_id=2, replica_groups=mesh['ctx'=8,'head'=4] {'ctx'}, dimensions={0}, use_global_device_ids=true | all-gather | bytes 360 | tf_op jit(solution)/shard_map/all_gather | solution.py:25
  139.1 1.1 fusion.86
  140.4 34.7 %all-gather.9.cloned.1.call-done = bf16[160,64,128]{2,1,0:T(8,128)(2,1)} async-done(((bf16[20,64,128]{2,1,0:T(8,128)(2,1)}), bf16[160,64,128]{2,1,0:T(8,128)(2,1)}) %all-gather.9.cloned.1.call-update) | async-done | bytes 2621456 | tf_op jit(solution)/shard_map/all_gather | solution.py:25
  175.2 8.4 %while.27 = (s32[]{:T(128)}, f32[1,20,64,128]{3,2,1,0:T(8,128)S(1)}, s32[]{:T(128)}, bf16[8,1,20]{2,1,0:T(2,128)(2,1)S(1)}, bf16[8,1,20,64,128]{4,3,2,1,0:T(8,12...) while((s32[]{:T(128)}, f32[1,20,64,128]{3,2,1,0:T(8,128)S(1)}, s32[]{:T(128)}, ...), condition=%wide.region_10.11_spmd, body=%wide.region_9.10_spmd.sunk | while | flops 491546 | bytes 1638755 | solution.py:40
  175.2 1.2 convert_add_fusion.5
  176.4 1.2 convert_add_fusion.5
  177.6 1.2 convert_add_fusion.5
  178.8 1.2 convert_add_fusion.5
  180.0 1.2 convert_add_fusion.5
  181.2 1.2 convert_add_fusion.5
  182.4 1.2 convert_add_fusion.5
  183.6 1.7 fusion.40
  186.1 4.0 %multiply_reduce_fusion = (f32[256,20]{0,1:T(8,128)S(1)}, f32[1,256,20,64]{1,3,2,0:T(8,128)S(1)}) fusion(f32[1,256,20,64]{1,3,2,0:T(8,128)S(1)} %bitcast.192, f32[1,256,20,64]{1,3,2,0:T(8,128)S(1)} %fusion.39, bf16[256,20,64]{0,2,1:T(8,128)(2,1)S(1)} %bitcast.190, f32[20,256]{1,0:T(8,128)S(1)} %copy-done.28, f32[256,256]{1,0:T(8,128)S(1)} %fusion.81, ...), kind=kOutput, calls=%fused_computation.63 | convolution fusion | flops 1013181440 | bytes 4976640 | tf_op jit(solution)/shard_map/bhts,bshp->bthp/dot_general | solution.py:128
  190.1 4.0 %multiply_reduce_fusion.1 = (f32[256,20]{0,1:T(8,128)S(1)}, f32[1,256,20,64]{1,3,2,0:T(8,128)S(1)}) fusion(f32[1,256,20,64]{1,3,2,0:T(8,128)S(1)} %bitcast.191, f32[1,256,20,64]{1,3,2,0:T(8,128)S(1)} %fusion.40, bf16[256,20,64]{0,2,1:T(8,128)(2,1)S(1)} %bitcast.188, f32[20,256]{1,0:T(8,128)S(1)} %copy-done.29, f32[256,256]{1,0:T(8,128)S(1)} %fusion.86, ...), kind=kOutput, calls=%fused_computation.69 | convolution fusion | flops 1013181440 | bytes 4976640 | tf_op jit(solution)/shard_map/bhts,bshp->bthp/dot_general | solution.py:128
  194.5 2.0 rev.10
  196.5 8.2 %fusion.53 = f32[512,2560]{1,0:T(8,128)} fusion(bf16[1280,2560]{1,0:T(8,128)(2,1)} %param.27, bf16[256,1280]{0,1:T(8,128)(2,1)S(1)} %rev.10, bf16[256,1280]{0,1:T(8,128)(2,1)S(1)} %bitcast.195), kind=kOutput, calls=%fused_computation.58 | convolution fusion | flops 3358064640 | bytes 13107200 | tf_op jit(solution)/shard_map/dot_general | solution.py:174
  204.8 3.4 %slice.133 = f32[256,2560]{1,0:T(8,128)} slice(f32[512,2560]{1,0:T(8,128)} %fusion.53), slice={[256:512], [0:2560]} | slice | bytes 5242880 | tf_op jit(solution)/shard_map/slice | solution.py:179
  208.2 18.6 %rev.11 = f32[256,2560]{1,0:T(8,128)S(1)} reverse(f32[256,2560]{1,0:T(8,128)} %slice.133), dimensions={1} | reverse | bytes 5242880 | tf_op jit(solution)/shard_map/rev | solution.py:179
  226.8 3.1 %fusion.18 = bf16[256,2560]{1,0:T(8,128)(2,1)} fusion(f32[256,2560]{1,0:T(8,128)S(1)} %rev.11, f32[512,2560]{1,0:T(8,128)} %fusion.53), kind=kLoop, calls=%fused_computation.27 | loop fusion | flops 1310720 | bytes 6553600 | tf_op jit(solution)/shard_map/convert_element_type | solution.py:181
  229.9 2.5 copy.115
  232.5 23.9 %reduce-scatter.4.cloned.1.call-done = bf16[640,256]{1,0:T(8,128)(2,1)} async-done(((bf16[2560,256]{1,0:T(8,128)(2,1)}), bf16[640,256]{1,0:T(8,128)(2,1)}) %reduce-scatter.4.cloned.1.call-update) | async-done | bytes 327696
  256.4 1.2 copy.116
  257.6 1.8 add_convert_fusion
  (161 shorter events, 19.6 us)
Async XLA Ops:
  6.5 1.8 copy-start
  6.5 133.8 %all-gather.7.cloned.1.call-start = ((), (), s32[]{:S(2)}) async-start(), calls=%async_computation.1 | async-start | bytes 2949120 | tf_op jit(solution)/shard_map/all_gather | solution.py:25
  8.3 37.9 %copy-start.33 = (f32[256]{0:T(256)}, f32[256]{0:T(256)S(1)}, u32[]{:S(2)}) copy-start(f32[256]{0:T(256)S(1)} %add_rsqrt_fusion.3) | copy-start | bytes 3076
  8.3 2.0 copy-start.2
  8.3 2.0 copy-start.39
  15.1 20.3 %copy-start.8 = (bf16[256,1280]{1,0:T(8,128)(2,1)}, bf16[256,1280]{1,0:T(8,128)(2,1)S(1)}, u32[]{:S(2)}) copy-start(bf16[256,1280]{1,0:T(8,128)(2,1)S(1)} %convolution_convert_fusion.3) | copy-start | bytes 1966084
  15.2 1.0 copy-start.6
  16.2 34.1 %collective-permute-start = (bf16[1,3,1536]{2,1,0:T(4,128)(2,1)S(1)}, bf16[1,3,1536]{2,1,0:T(4,128)(2,1)S(1)}, u32[]{:S(2)}, u32[]{:S(2)}) collective-permute-start(bf16[1,3,1536]{2,1,0:T(4,128)(2,1)S(1)} %slice.109), channel_id=1, source_target_pairs={{0,4},{4,8},{8,12},{12,16},{16,20},{20,24},{24,28},{1,5},{5,9},{9,... | collective-permute-start | bytes 27656 | tf_op jit(solution)/shard_map/ppermute | solution.py:17
  37.1 8.5 %copy-start.35 = (f32[256]{0:T(256)}, f32[256]{0:T(256)S(1)}, u32[]{:S(2)}) copy-start(f32[256]{0:T(256)S(1)} %add_rsqrt_fusion.2) | copy-start | bytes 3076
  37.1 2.0 copy-start.3
  39.1 4.9 %copy-start.14 = (bf16[256,256]{1,0:T(8,128)(2,1)}, bf16[256,256]{1,0:T(8,128)(2,1)S(1)}, u32[]{:S(2)}) copy-start(bf16[256,256]{1,0:T(8,128)(2,1)S(1)} %convolution_convert_fusion.4) | copy-start | bytes 393220
  44.0 2.2 copy-start.9
  44.0 1.6 copy-start.41
  44.0 1.6 copy-start.38
  44.0 1.6 copy-start.42
  44.1 2.1 copy-start.7
  44.1 6.2 %collective-permute-start.1 = (bf16[1,3,1536]{2,1,0:T(4,128)(2,1)S(1)}, bf16[1,3,1536]{2,1,0:T(4,128)(2,1)S(1)}, u32[]{:S(2)}, u32[]{:S(2)}) collective-permute-start(bf16[1,3,1536]{2,1,0:T(4,128)(2,1)S(1)} %slice.122), channel_id=1, source_target_pairs={{4,0},{8,4},{12,8},{16,12},{20,16},{24,20},{28,24},{5,1},{9,5},{13... | collective-permute-start | bytes 27656 | tf_op jit(solution)/shard_map/ppermute | solution.py:17
  46.3 18.7 %copy-start.18 = (f32[256,20]{1,0:T(8,128)}, f32[256,20]{1,0:T(8,128)S(1)}, u32[]{:S(2)}) copy-start(f32[256,20]{1,0:T(8,128)S(1)} %compare_select_fusion) | copy-start | bytes 61444
  46.3 2.1 copy-start.30
  46.3 3.8 %copy-start.32 = (f32[4,256]{1,0:T(4,128)S(1)}, f32[4,256]{1,0:T(4,128)}, u32[]{:S(2)}) copy-start(f32[4,256]{1,0:T(4,128)} %param.23) | copy-start | bytes 12292
  47.6 2.8 %copy-start.17 = (f32[256,20]{1,0:T(8,128)}, f32[256,20]{1,0:T(8,128)S(1)}, u32[]{:S(2)}) copy-start(f32[256,20]{1,0:T(8,128)S(1)} %get-tuple-element.213) | copy-start | bytes 61444
  47.6 3.4 %copy-start.15 = (bf16[256,256]{1,0:T(8,128)(2,1)S(1)}, bf16[256,256]{1,0:T(8,128)(2,1)}, u32[]{:S(2)}) copy-start(bf16[256,256]{1,0:T(8,128)(2,1)} %copy-done.14) | copy-start | bytes 393220
  48.2 0.6 copy-start.19
  50.3 0.6 copy-start.31
  56.6 5.8 %copy-start.5 = (bf16[1,256,1536]{2,1,0:T(8,128)(2,1)}, bf16[1,256,1536]{2,1,0:T(8,128)(2,1)S(1)}, u32[]{:S(2)}) copy-start(bf16[1,256,1536]{2,1,0:T(8,128)(2,1)S(1)} %get-tuple-element.207) | copy-start | bytes 2359300
  57.5 4.9 %copy-start.21 = (f32[256,20]{1,0:T(8,128)S(1)}, f32[256,20]{1,0:T(8,128)}, u32[]{:S(2)}) copy-start(f32[256,20]{1,0:T(8,128)} %get-tuple-element.212) | copy-start | bytes 61444
  62.4 112.7 %all-gather.9.cloned.1.call-start = ((), (), s32[]{:S(2)}) async-start(), calls=%async_computation.2 | async-start | bytes 2949120 | tf_op jit(solution)/shard_map/all_gather | solution.py:25
  63.1 0.6 copy-start.20
  65.8 19.3 %copy-start.16 = (f32[256,20]{1,0:T(8,128)S(1)}, f32[256,20]{1,0:T(8,128)}, u32[]{:S(2)}) copy-start(f32[256,20]{1,0:T(8,128)} %get-tuple-element.199) | copy-start | bytes 61444
  66.8 18.8 %copy-start.4 = (bf16[256,2560]{1,0:T(8,128)(2,1)S(1)}, bf16[256,2560]{1,0:T(8,128)(2,1)}, u32[]{:S(2)}) copy-start(bf16[256,2560]{1,0:T(8,128)(2,1)} %rev.9) | copy-start | bytes 3932164
  69.6 186.8 %reduce-scatter.4.cloned.1.call-start = ((), (), s32[]{:S(2)}) async-start(), calls=%async_computation.3 | async-start | bytes 1638400
  91.7 2.8 %copy-start.34 = (f32[256]{0:T(256)S(1)}, f32[256]{0:T(256)}, u32[]{:S(2)}) copy-start(f32[256]{0:T(256)} %copy-done.33) | copy-start | bytes 3076
  91.7 2.8 %copy-start.40 = (f32[2560]{0:T(1024)S(1)}, f32[2560]{0:T(1024)}, u32[]{:S(2)}) copy-start(f32[2560]{0:T(1024)} %param.17) | copy-start | bytes 30724
  99.3 1.6 copy-start.25
  99.4 1.6 copy-start.26
  99.4 1.6 copy-start.24
  99.4 1.6 copy-start.27
  99.4 1.6 copy-start.37
  99.4 23.5 %copy-start.36 = (bf16[1,20,1]{1,2,0:T(2,128)(2,1)S(1)}, bf16[1,20,1]{1,2,0:T(2,128)(2,1)}, u32[]{:S(2)}) copy-start(bf16[1,20,1]{1,2,0:T(2,128)(2,1)} %get-tuple-element.204) | copy-start | bytes 124
  175.2 8.4 %copy-start.23 = (f32[256,20]{0,1:T(8,128)S(1)}, f32[256,20]{0,1:T(8,128)}, u32[]{:S(2)}) copy-start(f32[256,20]{0,1:T(8,128)} %copy.87) | copy-start | bytes 61444
  183.6 1.7 copy-start.22
  183.6 2.4 copy-start.11
  183.6 2.4 copy-start.13
  183.6 2.4 copy-start.28
  186.0 4.0 %copy-start.10 = (bf16[1,256,1280]{1,2,0:T(8,128)(2,1)S(1)}, bf16[1,256,1280]{1,2,0:T(8,128)(2,1)}, u32[]{:S(2)}) copy-start(bf16[1,256,1280]{1,2,0:T(8,128)(2,1)} %copy.74) | copy-start | bytes 1966084
  186.0 4.0 %copy-start.12 = (f32[256,1280]{0,1:T(8,128)S(1)}, f32[256,1280]{0,1:T(8,128)}, u32[]{:S(2)}) copy-start(f32[256,1280]{0,1:T(8,128)} %copy.88) | copy-start | bytes 3932164
  186.1 4.0 %copy-start.29 = (f32[20,256]{1,0:T(8,128)S(1)}, f32[20,256]{1,0:T(8,128)}, u32[]{:S(2)}) copy-start(f32[20,256]{1,0:T(8,128)} %copy.80) | copy-start | bytes 61444
  229.9 29.4 %copy-start.1 = (bf16[2560,256]{1,0:T(8,128)(2,1)S(1)}, bf16[2560,256]{1,0:T(8,128)(2,1)}, u32[]{:S(2)}) copy-start(bf16[2560,256]{1,0:T(8,128)(2,1)} %param.20) | copy-start | bytes 3932164
Sparse Core Ops, SparseCore 0:
  62.5 57.0 all-gather.6
  121.8 53.2 all-gather.8
  232.6 23.7 reduce-scatter.3
where the time goes:
time: 268 us; the launch traced here: 266 us
  local copies, waits for them, and re-layouts  70.7 us (26%)
  waiting for transfers between devices  58.6 us (22%)
  matrix products  51.3 us (19%)
  blocking collectives  38.1 us (14%)
  other arithmetic  26.4 us (10%)
  between operations  13.9 us (5%)
  starting transfers between devices  6.56 us (2%)
    all_gather x2, blocking collectives, prefix(): lax.all_gather(a.astype(kind), axis)  38.1 us
    all_gather x2, waiting for transfers between devices, prefix(): lax.all_gather(a.astype(kind), axis)  34.7 us
    unnamed x4, waiting for transfers between devices  24 us
    rev x1, local copies, waits for them, and re-layouts, per_device(): partial_sum = projected[:row_count] + projected[row_count:, ::-1]  18.6 us
    rev x1, local copies, waits for them, and re-layouts, per_device(): hidden[::-1, ::-1][None]  14.4 us
    dot_general x2, matrix products, mixer(): jnp.dot(normed, z_weight, preferred_element_type=jnp.float32)  10.8 us
    unnamed x97, local copies, waits for them, and re-layouts  10 us
    dot_general x2, matrix products, mixer(): jnp.dot(normed, x_weight, preferred_element_type=jnp.float32)  9.61 us
  transfers between devices with their start and end apart: 5, of which 2 were waited for; matrix products, arithmetic and copies ran while one was open for 25% of the time, Pallas kernels for 0%

commit v1 on v0

v1 whole, which is shorter than its diff:
```python
import functools

import jax
import jax.numpy as jnp
from jax import lax
from jax.experimental import pallas as pl
from jax.experimental.pallas import tpu as pltpu
from jax.sharding import PartitionSpec as P

HEAD_DIM = 64
STATE = 128
GROUP = 256
LANES = 128
HALO = 16
epsilon = 1e-05
highest = lax.Precision.HIGHEST
MESH = pl.DeviceIdType.MESH
f32 = jnp.float32
bf16 = jnp.bfloat16


def iota(shape, dim):
    return lax.broadcasted_iota(jnp.int32, shape, dim)


def dot(a, b, precision=None):
    return jnp.dot(a, b, preferred_element_type=f32, precision=precision)


def silu(v):
    return v / (1.0 + jnp.exp(-v))


def anti(size):
    return (iota((size, size), 0) + iota((size, size), 1) == size - 1).astype(bf16)


def spread(group):
    head = group * (GROUP // HEAD_DIM) + iota((LANES, GROUP), 1) // HEAD_DIM
    return (iota((LANES, GROUP), 0) == head).astype(f32)


def conv_fwd(ext, taps, rows):
    out = taps[0:1] * ext[HALO - 3 : HALO - 3 + rows]
    for k in range(1, 4):
        out = out + taps[k : k + 1] * ext[HALO - 3 + k : HALO - 3 + k + rows]
    return silu(out).astype(bf16)


def conv_bwd(ext, taps, rows):
    out = taps[0:1] * ext[3 : 3 + rows]
    for k in range(1, 4):
        out = out + taps[k : k + 1] * ext[3 - k : 3 - k + rows]
    return silu(out).astype(bf16)


def first_kernel(
    h_ref, prev_ref, next_ref, gain_ref, bcw_ref, dtw_ref, bck_ref, dtb_ref, rate_ref, xw_ref, xk_ref,
    n_ref, bc_ref, delta_ref, cum_ref, cumt_ref, x_ref, s_ref, dec_ref,
    next_n, wend, pad,
):
    rows, width = h_ref.shape
    ext = rows + HALO
    group = pl.program_id(0)

    @pl.when(group == 0)
    def _():
        gain = gain_ref[...]
        blocks = width // GROUP
        flip = anti(GROUP)

        def turned(ref):
            parts = [
                dot(ref[:, (blocks - 1 - j) * GROUP : (blocks - j) * GROUP], flip) for j in range(blocks)
            ]
            return jnp.concatenate(parts, axis=1)

        def scale(u):
            return lax.rsqrt(jnp.mean(u * u, axis=1, keepdims=True) + epsilon)

        here = h_ref[...].astype(f32)
        factor = scale(here)
        n_ref[HALO:ext, :] = (here * factor * gain).astype(bf16)
        n_ref[ext : ext + rows, :] = (turned(h_ref) * factor * gain).astype(bf16)
        prior = prev_ref[...].astype(f32)
        n_ref[0:HALO, :] = (prior * scale(prior) * gain).astype(bf16)
        later = turned(next_ref)
        n_ref[ext + rows :, :] = (later * scale(later) * gain).astype(bf16)

        bc_in = dot(n_ref[...], bcw_ref[...]).astype(bf16).astype(f32)
        bc_ref[0] = conv_fwd(bc_in[:ext], bck_ref[...], rows)
        bc_ref[1] = conv_bwd(bc_in[ext:], bck_ref[...], rows)

        raw = dot(n_ref[HALO : ext + rows, :], dtw_ref[...]) + dtb_ref[...]
        step = jnp.maximum(raw, 0.0) + jnp.log1p(jnp.exp(-jnp.abs(raw)))
        decay = -step * jnp.exp(rate_ref[...])
        heads = raw.shape[1]
        pad[...] = jnp.zeros_like(pad)
        pad[0, :, 0:heads] = step
        pad[1, :, 0:heads] = decay
        tri = iota((rows, rows), 0) >= iota((rows, rows), 1)
        for d in range(2):
            mine = slice(d * rows, (d + 1) * rows)
            mask = tri if d == 0 else iota((rows, rows), 0) <= iota((rows, rows), 1)
            cum = dot(mask.astype(f32), pad[1, mine, :], highest)
            end = cum[rows - 1 : rows] if d == 0 else cum[0:1]
            delta_ref[d] = pad[0, mine, :]
            cum_ref[d] = cum
            cumt_ref[d] = cum.T
            wend[d] = jnp.exp(end - cum) * pad[0, mine, :]
            next_n[d] = jnp.broadcast_to(jnp.exp(end), (8, LANES))

    x_in = dot(n_ref[...], xw_ref[...]).astype(bf16).astype(f32)
    taps = xk_ref[...]
    hot = spread(group)
    for d in range(2):
        x_conv = conv_fwd(x_in[:ext], taps, rows) if d == 0 else conv_bwd(x_in[ext:], taps, rows)
        x_ref[d, 0] = x_conv
        weighted = (x_conv.astype(f32) * dot(wend[d], hot, highest)).astype(bf16)
        s_ref[d, 0] = lax.dot_general(
            bc_ref[d, :, :STATE], weighted, (((0,), (0,)), ((), ())), preferred_element_type=f32
        ).astype(bf16)
        dec_ref[d, 0] = dot(next_n[d], hot, highest)


def second_kernel(
    n_ctx, axes,
    n_ref, bc_ref, delta_ref, cum_ref, cumt_ref, x_ref, s_ref, dec_ref, gain_ref, h_ref, zw_hbm, ow_hbm,
    out_ref,
    zw, ow, z_buf, y_buf, gated, gram, carry, send_buf, one_send, one_recv, two_send, two_recv,
    zw_sem, ow_sem, c_send, c_recv, r_send, r_recv,
):
    ctx_axis, head_axis = axes
    me = lax.axis_index(ctx_axis)
    place = lax.axis_index(head_axis)
    groups = x_ref.shape[1]
    rows = x_ref.shape[2]
    block = out_ref.shape[1]
    core = lax.rem(place, 2)
    side = place // 2
    sibling = side * 2 + (1 - core)
    across = (1 - side) * 2 + core

    z_copies = [
        pltpu.make_async_copy(zw_hbm.at[:, pl.ds(g * GROUP, GROUP)], zw.at[g], zw_sem.at[g])
        for g in range(groups)
    ]
    o_copy = pltpu.make_async_copy(ow_hbm, ow, ow_sem)
    for copy in z_copies:
        copy.start()
    o_copy.start()

    barrier = pltpu.get_barrier_semaphore()
    for peer in (sibling, across):
        pl.semaphore_signal(barrier, inc=1, device_id={head_axis: peer}, device_id_type=MESH)

    @pl.when(me > 0)
    def _():
        pl.semaphore_signal(barrier, inc=1, device_id={ctx_axis: me - 1}, device_id_type=MESH)

    @pl.when(me < n_ctx - 1)
    def _():
        pl.semaphore_signal(barrier, inc=1, device_id={ctx_axis: me + 1}, device_id_type=MESH)

    ends = jnp.where(me > 0, 1, 0) + jnp.where(me < n_ctx - 1, 1, 0)
    pl.semaphore_wait(barrier, 2 + ends)

    def chain_copy(d, g, target):
        return pltpu.make_async_remote_copy(
            src_ref=send_buf.at[d, g],
            dst_ref=carry.at[d, g],
            send_sem=c_send.at[d, g],
            recv_sem=c_recv.at[d, g],
            device_id={ctx_axis: target},
            device_id_type=MESH,
        )

    def chain(d):
        target = me + 1 - 2 * d
        source = me - 1 + 2 * d
        has_source = jnp.logical_and(source >= 0, source < n_ctx)
        has_target = jnp.logical_and(target >= 0, target < n_ctx)

        def one(g, _):
            @pl.when(has_source)
            def _():
                chain_copy(d, g, source).wait_recv()

            @pl.when(jnp.logical_not(has_source))
            def _():
                carry[d, g] = jnp.zeros_like(carry[d, g])

            @pl.when(has_target)
            def _():
                total = carry[d, g].astype(f32) * dec_ref[d, g, 0:1, :] + s_ref[d, g].astype(f32)
                send_buf[d, g] = total.astype(bf16)
                chain_copy(d, g, target).start()

            return 0

        lax.fori_loop(0, groups, one, 0)

    def unit(g, _):
        pltpu.make_async_copy(zw_hbm.at[:, pl.ds(0, GROUP)], zw.at[g], zw_sem.at[g]).wait()
        z_buf[g] = dot(n_ref[HALO : HALO + 2 * rows, :], zw[g]).astype(bf16)
        hot = spread(g)
        lane_head = iota((rows, GROUP), 1) // HEAD_DIM
        for d in range(2):
            scaled = x_ref[d, g].astype(f32) * dot(delta_ref[d], hot, highest)
            cols = dot(cum_ref[d], hot, highest)
            parts, values = [], []
            for j in range(GROUP // HEAD_DIM):
                column = cols[:, j * HEAD_DIM : j * HEAD_DIM + 1]
                row = cumt_ref[d, pl.ds(g * (GROUP // HEAD_DIM) + j, 1), :]
                parts.append((jnp.exp(jnp.minimum(column - row, 0.0)) * gram[d]).astype(bf16))
                values.append(jnp.where(lane_head == j, scaled, 0.0).astype(bf16))
            y_buf[g, d] = dot(jnp.concatenate(parts, axis=1), jnp.concatenate(values, axis=0))
        return 0

    late = me >= n_ctx // 2
    first = jnp.where(late, 1, 0)
    distance = jnp.where(late, n_ctx - 1 - me, me)
    before = jnp.minimum(groups, distance + distance // 2)

    for d in range(2):
        full = lax.dot_general(
            bc_ref[d, :, STATE:], bc_ref[d, :, :STATE], (((1,), (1,)), ((), ())), preferred_element_type=f32
        )
        ahead = iota((rows, rows), 0) - iota((rows, rows), 1)
        gram[d] = jnp.where(ahead >= 0 if d == 0 else ahead <= 0, full, 0.0)

    lax.fori_loop(0, before, unit, 0)
    chain(first)
    lax.fori_loop(before, groups, unit, 0)
    chain(1 - first)

    same = iota((GROUP, GROUP), 0) // HEAD_DIM == iota((GROUP, GROUP), 1) // HEAD_DIM
    average = jnp.where(same, 1.0 / HEAD_DIM, 0.0).astype(bf16)
    growth = [jnp.exp(cum_ref[d]) for d in range(2)]
    for g in range(groups):
        hot = spread(g)
        for d in range(2):
            carried = dot(bc_ref[d, :, STATE:], carry[d, g]) * dot(growth[d], hot, highest)
            value = (y_buf[g, d] + carried) * silu(z_buf[g, d * rows : (d + 1) * rows].astype(f32))
            square = value * value
            high = square.astype(bf16)
            low = (square - high.astype(f32)).astype(bf16)
            mean_sq = dot(high, average) + dot(low, average)
            lanes = slice(g * GROUP, (g + 1) * GROUP)
            gated[d, :, lanes] = (
                value * lax.rsqrt(mean_sq + epsilon) * gain_ref[:, lanes]
            ).astype(bf16)

    o_copy.wait()
    flip = anti(LANES)
    blocks = ow_hbm.shape[1] // block

    def project(which):
        mine = pl.multiple_of(which * block, LANES)
        other = pl.multiple_of((blocks - 1 - which) * block, LANES)
        ahead = dot(gated[0], ow[:, pl.ds(mine, block)])
        back = dot(gated[1], ow[:, pl.ds(other, block)]).astype(bf16)
        count = block // LANES
        turned = [
            dot(back[:, (count - 1 - j) * LANES : (count - j) * LANES], flip) for j in range(count)
        ]
        return ahead + jnp.concatenate(turned, axis=1)

    def near(slot):
        return pltpu.make_async_remote_copy(
            src_ref=one_send.at[slot],
            dst_ref=one_recv.at[slot],
            send_sem=r_send.at[slot],
            recv_sem=r_recv.at[slot],
            device_id={head_axis: sibling},
            device_id_type=MESH,
        )

    far = pltpu.make_async_remote_copy(
        src_ref=two_send,
        dst_ref=two_recv,
        send_sem=r_send.at[2],
        recv_sem=r_recv.at[2],
        device_id={head_axis: across},
        device_id_type=MESH,
    )
    one_send[0] = project((1 - side) * 2 + (1 - core)).astype(bf16)
    near(0).start()
    partial = project(across)
    near(0).wait_recv()
    two_send[...] = (partial + one_recv[0].astype(f32)).astype(bf16)
    far.start()
    one_send[1] = project(sibling).astype(bf16)
    near(1).start()
    partial = project(place)
    residual = h_ref[:, pl.ds(pl.multiple_of(place * block, LANES), block)].astype(f32)
    near(1).wait_recv()
    partial = partial + one_recv[1].astype(f32)
    far.wait_recv()
    out_ref[...] = (residual + (partial + two_recv[...].astype(f32))).astype(out_ref.dtype)
    near(0).wait_send()
    near(1).wait_send()
    far.wait_send()

    def drain(g, _):
        @pl.when(me < n_ctx - 1)
        def _():
            chain_copy(0, g, me + 1).wait_send()

        @pl.when(me > 0)
        def _():
            chain_copy(1, g, me - 1).wait_send()

        return 0

    lax.fori_loop(0, groups, drain, 0)


def per_device(
    mesh,
    hidden,
    norm_gain,
    x_weight,
    z_weight,
    bc_weight,
    dt_weight,
    x_kernel,
    bc_kernel,
    dt_bias,
    log_rate,
    out_gain,
    out_weight,
):
    n_ctx = mesh.shape["ctx"]
    n_head = mesh.shape["head"]
    rows, width = hidden.shape
    inner = x_weight.shape[1]
    groups = inner // GROUP
    heads = inner // HEAD_DIM
    prev = lax.ppermute(hidden[rows - HALO :], "ctx", [(i, i + 1) for i in range(n_ctx - 1)])
    follow = lax.ppermute(hidden[:HALO], "ctx", [(i + 1, i) for i in range(n_ctx - 1)])

    def whole(*shape):
        return pl.BlockSpec(shape, lambda g: (0,) * len(shape))

    long = 2 * (rows + HALO)
    shapes = [
        jax.ShapeDtypeStruct((long, width), bf16),
        jax.ShapeDtypeStruct((2, rows, 2 * STATE), bf16),
        jax.ShapeDtypeStruct((2, rows, LANES), f32),
        jax.ShapeDtypeStruct((2, rows, LANES), f32),
        jax.ShapeDtypeStruct((2, LANES, rows), f32),
        jax.ShapeDtypeStruct((2, groups, rows, GROUP), bf16),
        jax.ShapeDtypeStruct((2, groups, STATE, GROUP), bf16),
        jax.ShapeDtypeStruct((2, groups, 8, GROUP), f32),
    ]
    made = pl.pallas_call(
        first_kernel,
        grid=(groups,),
        out_shape=shapes,
        in_specs=[
            whole(rows, width),
            whole(HALO, width),
            whole(HALO, width),
            whole(1, width),
            whole(width, 2 * STATE),
            whole(width, heads),
            whole(4, 2 * STATE),
            whole(1, heads),
            whole(1, heads),
            pl.BlockSpec((width, GROUP), lambda g: (0, g)),
            pl.BlockSpec((4, GROUP), lambda g: (0, g)),
        ],
        out_specs=[
            whole(long, width),
            whole(2, rows, 2 * STATE),
            whole(2, rows, LANES),
            whole(2, rows, LANES),
            whole(2, LANES, rows),
            pl.BlockSpec((2, 1, rows, GROUP), lambda g: (0, g, 0, 0)),
            pl.BlockSpec((2, 1, STATE, GROUP), lambda g: (0, g, 0, 0)),
            pl.BlockSpec((2, 1, 8, GROUP), lambda g: (0, g, 0, 0)),
        ],
        scratch_shapes=[
            pltpu.VMEM((2, 8, LANES), f32),
            pltpu.VMEM((2, rows, LANES), f32),
            pltpu.VMEM((2, 2 * rows, LANES), f32),
        ],
        compiler_params=pltpu.CompilerParams(vmem_limit_bytes=48 * 2**20),
        cost_estimate=pl.CostEstimate(flops=4_200_000_000, bytes_accessed=14_000_000, transcendentals=2_000_000),
        name="project_x",
    )(
        hidden,
        prev,
        follow,
        norm_gain[None],
        bc_weight,
        dt_weight,
        bc_kernel,
        dt_bias[None],
        log_rate[None],
        x_weight,
        x_kernel,
    )
    block = width // n_head
    vmem = pl.BlockSpec(memory_space=pltpu.VMEM)
    hbm = pl.BlockSpec(memory_space=pl.ANY)
    return pl.pallas_call(
        functools.partial(second_kernel, n_ctx, ("ctx", "head")),
        out_shape=jax.ShapeDtypeStruct((rows, block), hidden.dtype),
        in_specs=[vmem] * 10 + [hbm] * 2,
        out_specs=vmem,
        scratch_shapes=[
            pltpu.VMEM((groups, width, GROUP), bf16),
            pltpu.VMEM((inner, width), bf16),
            pltpu.VMEM((groups, 2 * rows, GROUP), bf16),
            pltpu.VMEM((groups, 2, rows, GROUP), f32),
            pltpu.VMEM((2, rows, inner), bf16),
            pltpu.VMEM((2, rows, rows), f32),
            pltpu.VMEM((2, groups, STATE, GROUP), bf16),
            pltpu.VMEM((2, groups, STATE, GROUP), bf16),
            pltpu.VMEM((2, rows, block), bf16),
            pltpu.VMEM((2, rows, block), bf16),
            pltpu.VMEM((rows, block), bf16),
            pltpu.VMEM((rows, block), bf16),
            pltpu.SemaphoreType.DMA((groups,)),
            pltpu.SemaphoreType.DMA,
            pltpu.SemaphoreType.DMA((2, groups)),
            pltpu.SemaphoreType.DMA((2, groups)),
            pltpu.SemaphoreType.DMA((3,)),
            pltpu.SemaphoreType.DMA((3,)),
        ],
        compiler_params=pltpu.CompilerParams(
            collective_id=0, has_side_effects=True, vmem_limit_bytes=56 * 2**20
        ),
        cost_estimate=pl.CostEstimate(flops=8_000_000_000, bytes_accessed=20_000_000, transcendentals=3_000_000),
        name="mix_and_project",
    )(*made, out_gain[None], hidden, z_weight, out_weight)


def solution(mesh):
    return jax.shard_map(
        functools.partial(per_device, mesh),
        mesh=mesh,
        in_specs=(
            P("ctx", None),
            P(),
            P(None, "head"),
            P(None, "head"),
            P(),
            P(None, "head"),
            P(None, "head"),
            P(),
            P("head"),
            P("head"),
            P("head"),
            P("head", None),
        ),
        out_specs=P("ctx", "head"),
        check_vma=False,
    )
```

time: 268 us -> 108 us (0.40)
  Pallas kernels: 0 us -> 84 us
  waiting for transfers between devices: 58.6 us -> 1.76 us
  local copies, waits for them, and re-layouts: 70.7 us -> 15.3 us
  matrix products: 51.3 us -> 0 us
  blocking collectives: 38.1 us -> 0 us
  other arithmetic: 26.4 us -> 0 us
  between operations: 13.9 us -> 0.04 us
    pallas_call x0 -> x2, Pallas kernels: none -> 84 us  [the longest x1 64.4 us: per_device(): pl.pallas_call(functools.partial(second_kernel, n_ctx, ('ctx', 'head')),...]
    dot_general x17 -> x0, matrix products: 51.3 us -> none  [the longest x2 10.8 us: mixer(): jnp.dot(normed, z_weight, preferred_element_type=jnp.float32)]
    all_gather x2 -> x0, blocking collectives: 38.1 us -> none  [prefix(): lax.all_gather(a.astype(kind), axis)]
    rev x3 -> x0, local copies, waits for them, and re-layouts: 35.1 us -> none  [the longest x1 18.6 us: per_device(): partial_sum = projected[:row_count] + projected[row_count:, ::-1]]
    all_gather x2 -> x0, waiting for transfers between devices: 34.7 us -> none  [prefix(): lax.all_gather(a.astype(kind), axis)]
    unnamed x4 -> x0, waiting for transfers between devices: 24 us -> none
    convert_element_type x11 -> x0, other arithmetic: 11.1 us -> none  [the longest x1 5.63 us: conv_silu(): return jax.nn.silu(running).astype(jnp.bfloat16)]
    mul x7 -> x0, local copies, waits for them, and re-layouts: 10.6 us -> none  [the longest x2 4.31 us: mixer(): jax.nn.silu(z_in.astype(jnp.float32))]
  transfers between devices with their start and end apart: 5 -> 2, of which waited for: 2 -> 1; matrix products, arithmetic and copies ran while one was open for 25% -> 3% of each run, Pallas kernels for 0% -> 0%
where the time goes in v1:
time: 108 us; the launch traced here: 107 us
  Pallas kernels  84 us (78%)
  local copies, waits for them, and re-layouts  15.3 us (14%)
  starting transfers between devices  6.17 us (6%)
  waiting for transfers between devices  1.76 us (2%)
    pallas_call x1, Pallas kernels, per_device(): pl.pallas_call(functools.partial(second_kernel, n_ctx, ('ctx', 'head')),...  64.4 us
    pallas_call x1, Pallas kernels, per_device(): pl.pallas_call(first_kernel, grid=(groups,), out_shape=shapes, in_specs=[...  19.6 us
    unnamed x26, local copies, waits for them, and re-layouts  12.4 us
    ppermute x1, starting transfers between devices, per_device(): lax.ppermute(hidden[rows - HALO:], 'ctx', [(i, i + 1) for i in range(n_ct...  4.88 us
  transfers between devices with their start and end apart: 2, of which 1 were waited for; matrix products, arithmetic and copies ran while one was open for 3% of the time, Pallas kernels for 0%

profile of v1, /device:TPU:0, one launch (start us, length us, event | category | flops | bytes accessed | tf_op | source)
XLA Modules:
  0.0 107.3 jit_solution(11896135724059490919)
XLA Ops:
  0.0 0.9 fusion
  0.9 4.9 %collective-permute-start = (bf16[16,2560]{1,0:T(8,128)(2,1)S(1)}, bf16[16,2560]{1,0:T(8,128)(2,1)S(1)}, u32[]{:S(2)}, u32[]{:S(2)}) collective-permute-start(bf16[16,2560]{1,0:T(8,128)(2,1)S(1)} %get-tuple-element.22), channel_id=1, source_target_pairs={{0,4},{4,8},{8,12},{12,16},{16,20},{20,24},{24,28},{1,5},{5,9},{9,... | collective-permute-start | bytes 245768 | tf_op jit(solution)/shard_map/ppermute | solution.py:340
  5.8 1.3 %collective-permute-start.1 = (bf16[16,2560]{1,0:T(8,128)(2,1)S(1)}, bf16[16,2560]{1,0:T(8,128)(2,1)S(1)}, u32[]{:S(2)}, u32[]{:S(2)}) collective-permute-start(bf16[16,2560]{1,0:T(8,128)(2,1)S(1)} %get-tuple-element.21), channel_id=1, source_target_pairs={{4,0},{8,4},{12,8},{16,12},{20,16},{24,20},{28,24},{5,1},{9,5},{13... | collective-permute-start | bytes 245768 | tf_op jit(solution)/shard_map/ppermute | solution.py:341
  7.1 1.3 %copy.13.dtw_ref = bf16[2560,20]{1,0:T(8,128)(2,1)S(1)} copy(bf16[2560,20]{0,1:T(8,128)(2,1)} %param.17) | data formatting | bytes 204800 | tf_op args[5]
  8.4 0.7 broadcast_in_dim.12.gain_ref
  9.1 1.3 %broadcast_in_dim.15.gain_ref = f32[1,1280]{1,0:T(1,128)} reshape(f32[1280]{0:T(1024)} %param.22) | data formatting | bytes 10240 | tf_op jit(solution)/shard_map/broadcast_in_dim | solution.py:438
  10.4 0.0 collective-permute-done.prev_ref
  10.4 1.8 %collective-permute-done.1.next_ref = bf16[16,2560]{1,0:T(8,128)(2,1)S(1)} collective-permute-done((bf16[16,2560]{1,0:T(8,128)(2,1)S(1)}, bf16[16,2560]{1,0:T(8,128)(2,1)S(1)}, u32[]{:S(2)}, u32[]{:S(2)}) %collective-permute-start.1) | collective-permute-done | bytes 81952 | tf_op jit(solution)/shard_map/ppermute | solution.py:341
  12.2 0.0 copy-start
  12.2 1.3 %copy-done = bf16[256,2560]{1,0:T(8,128)(2,1)S(1)} copy-done((bf16[256,2560]{1,0:T(8,128)(2,1)S(1)}, bf16[256,2560]{1,0:T(8,128)(2,1)}, u32[]{:S(2)}) %copy-start) | copy-done | bytes 1310744
  13.5 0.0 copy-start.1
  13.5 0.7 copy-done.1
  14.2 0.0 copy-start.2
  14.2 0.7 copy-done.2
  14.9 0.0 copy-start.3
  14.9 0.7 copy-done.3
  15.5 0.0 copy-start.4
  15.6 0.7 copy-done.4
  16.2 19.6 %project_x.1 = (bf16[544,2560]{1,0:T(8,128)(2,1)}, bf16[2,256,256]{2,1,0:T(8,128)(2,1)S(1)}, f32[2,256,128]{2,1,0:T(8,128)S(1)}, f32[2,256,128]{2,1,0:T(8,128)S(...) custom-call(bf16[256,2560]{1,0:T(8,128)(2,1)S(1)} %copy-done, ...), custom_call_target="tpu_custom_call" | custom-call | flops 4200000000 | bytes 14000000 | tf_op jit(solution)/shard_map/project_x/pallas_call | solution.py:357
  35.8 0.0 copy-start.5
  35.8 1.1 copy-done.5
  36.9 0.0 copy-start.6
  36.9 0.8 copy-done.6
  37.7 0.0 copy-start.7
  37.7 0.7 copy-done.7
  38.4 0.0 copy-start.8
  38.4 0.7 copy-done.8
  39.1 0.0 copy-start.9
  39.1 0.7 copy-done.9
  39.8 0.0 copy-start.10
  39.8 0.7 copy-done.10
  40.5 0.0 copy-start.11
  40.5 0.6 copy-done.11
  41.1 64.4 %mix_and_project.1 = bf16[256,640]{1,0:T(8,128)(2,1)} custom-call(bf16[544,2560]{1,0:T(8,128)(2,1)} %get-tuple-element.13.n_ref, bf16[2,256,256]{2,1,0:T(8,128)(2,1)} %copy-done.7, f32[2,256,128]{2,1,0:T(8,128)} %copy-done.8, f32[2,256,128]{2,1,0:T(8,128)} %copy-done.9, f32[2,128,256]{2,1,0:T(8,128)} %copy-done.10, bf16[2,5,256,256]{3,2,1,0:T(8,128)(2,1)} %copy-done.5, ...), custom_call_target="tpu_custom_call" | custom-call | flops 8000000000 | bytes 20000000 | tf_op jit(solution)/shard_map/mix_and_project/pallas_call | solution.py:408
  105.6 1.7 %copy.15 = bf16[256,640]{1,0:T(8,128)(2,1)} copy(bf16[256,640]{1,0:T(8,128)(2,1)} %mix_and_project.1) | data formatting | bytes 655360
Async XLA Ops:
  0.9 9.5 %collective-permute-start = (bf16[16,2560]{1,0:T(8,128)(2,1)S(1)}, bf16[16,2560]{1,0:T(8,128)(2,1)S(1)}, u32[]{:S(2)}, u32[]{:S(2)}) collective-permute-start(bf16[16,2560]{1,0:T(8,128)(2,1)S(1)} %get-tuple-element.22), channel_id=1, source_target_pairs={{0,4},{4,8},{8,12},{12,16},{16,20},{20,24},{24,28},{1,5},{5,9},{9,... | collective-permute-start | bytes 245768 | tf_op jit(solution)/shard_map/ppermute | solution.py:340
  5.8 6.3 %collective-permute-start.1 = (bf16[16,2560]{1,0:T(8,128)(2,1)S(1)}, bf16[16,2560]{1,0:T(8,128)(2,1)S(1)}, u32[]{:S(2)}, u32[]{:S(2)}) collective-permute-start(bf16[16,2560]{1,0:T(8,128)(2,1)S(1)} %get-tuple-element.21), channel_id=1, source_target_pairs={{4,0},{8,4},{12,8},{16,12},{20,16},{24,20},{28,24},{5,1},{9,5},{13... | collective-permute-start | bytes 245768 | tf_op jit(solution)/shard_map/ppermute | solution.py:341
  12.2 1.3 %copy-start = (bf16[256,2560]{1,0:T(8,128)(2,1)S(1)}, bf16[256,2560]{1,0:T(8,128)(2,1)}, u32[]{:S(2)}) copy-start(bf16[256,2560]{1,0:T(8,128)(2,1)} %h_ref.3) | copy-start | bytes 3932164
  13.5 0.7 copy-start.1
  14.2 0.7 copy-start.2
  14.9 0.7 copy-start.3
  15.5 0.7 copy-start.4
  35.8 1.1 %copy-start.5 = (bf16[2,5,256,256]{3,2,1,0:T(8,128)(2,1)}, bf16[2,5,256,256]{3,2,1,0:T(8,128)(2,1)S(1)}, u32[]{:S(2)}) copy-start(bf16[2,5,256,256]{3,2,1,0:T(8,128)(2,1)S(1)} %get-tuple-element.18.x_ref) | copy-start | bytes 3932164
  36.9 0.8 copy-start.6
  37.7 0.7 copy-start.7
  38.4 0.7 copy-start.8
  39.1 0.7 copy-start.9
  39.8 0.7 copy-start.10
  40.5 0.6 copy-start.11

commit v2 on v1

v2 whole, which is shorter than its diff:
```python
import functools

import jax
import jax.numpy as jnp
from jax import lax
from jax.experimental import pallas as pl
from jax.experimental.pallas import tpu as pltpu
from jax.sharding import PartitionSpec as P

HEAD_DIM = 64
STATE = 128
GROUP = 256
LANES = 128
HALO = 16
epsilon = 1e-05
highest = lax.Precision.HIGHEST
MESH = pl.DeviceIdType.MESH
f32 = jnp.float32
bf16 = jnp.bfloat16


def iota(shape, dim):
    return lax.broadcasted_iota(jnp.int32, shape, dim)


def dot(a, b, precision=None):
    return jnp.dot(a, b, preferred_element_type=f32, precision=precision)


def silu(v):
    return v / (1.0 + jnp.exp(-v))


def anti(size):
    return (iota((size, size), 0) + iota((size, size), 1) == size - 1).astype(bf16)


def spread(group):
    head = group * (GROUP // HEAD_DIM) + iota((LANES, GROUP), 1) // HEAD_DIM
    return (iota((LANES, GROUP), 0) == head).astype(f32)


def conv_fwd(ext, taps, rows):
    out = taps[0:1] * ext[HALO - 3 : HALO - 3 + rows]
    for k in range(1, 4):
        out = out + taps[k : k + 1] * ext[HALO - 3 + k : HALO - 3 + k + rows]
    return silu(out).astype(bf16)


def conv_bwd(ext, taps, rows):
    out = taps[0:1] * ext[3 : 3 + rows]
    for k in range(1, 4):
        out = out + taps[k : k + 1] * ext[3 - k : 3 - k + rows]
    return silu(out).astype(bf16)


def kernel(
    n_ctx, axes,
    gain_ref, dtw_ref, xk_ref, bck_ref, dtb_ref, rate_ref, out_gain_ref, h_hbm, xw_hbm, zw_hbm, bcw_hbm, ow_hbm,
    out_ref,
    h_buf, prev, follow, bcw, xw, zw, ow, n_buf, pad, bc, delta, cum, cumt, wend, dec, pair_dec,
    x_buf, z_buf, y_buf, gated, gram, state, pair_state, chain_in, carry, send_buf,
    one_send, one_recv, two_send, two_recv,
    in_sem, xw_sem, zw_sem, halo_send, halo_recv, d_send, d_recv, p_send, p_recv, c_send, c_recv, f_send, f_recv,
    r_send, r_recv,
):
    ctx_axis, head_axis = axes
    me = lax.axis_index(ctx_axis)
    place = lax.axis_index(head_axis)
    rows, width = h_buf.shape
    groups = x_buf.shape[1]
    block = out_ref.shape[1]
    ext = rows + HALO
    core = lax.rem(place, 2)
    side = place // 2
    sibling = side * 2 + (1 - core)
    across = (1 - side) * 2 + core
    other = lax.rem(me, 2)
    mine = 1 - other
    partner = me + 1 - 2 * other
    target = me + 2 - 4 * mine
    source = me - 2 + 4 * mine
    has_source = jnp.logical_and(source >= 0, source < n_ctx)
    has_target = jnp.logical_and(target >= 0, target < n_ctx)
    their_source = partner - 2 + 4 * other
    other_source = jnp.logical_and(their_source >= 0, their_source < n_ctx)

    def weight_copy(hbm, buf, sem, g):
        lanes = pl.ds(pl.multiple_of(g * GROUP, GROUP), GROUP)
        return pltpu.make_async_copy(hbm.at[:, lanes], buf.at[g], sem.at[g])

    h_copy = pltpu.make_async_copy(h_hbm, h_buf, in_sem.at[0])
    bc_copy = pltpu.make_async_copy(bcw_hbm, bcw, in_sem.at[1])
    o_copy = pltpu.make_async_copy(ow_hbm, ow, in_sem.at[2])
    h_copy.start()
    bc_copy.start()
    for g in range(groups):
        weight_copy(xw_hbm, xw, xw_sem, g).start()
    for g in range(groups):
        weight_copy(zw_hbm, zw, zw_sem, g).start()
    o_copy.start()

    barrier = pltpu.get_barrier_semaphore()
    for peer in (sibling, across):
        pl.semaphore_signal(barrier, inc=1, device_id={head_axis: peer}, device_id_type=MESH)
    peers = 2
    for hop in (-2, -1, 1, 2):
        present = jnp.logical_and(me + hop >= 0, me + hop < n_ctx)
        peers = peers + jnp.where(present, 1, 0)

        @pl.when(present)
        def _():
            pl.semaphore_signal(barrier, inc=1, device_id={ctx_axis: me + hop}, device_id_type=MESH)

    pl.semaphore_wait(barrier, peers)

    def remote(src, dst, send, recv, to):
        return pltpu.make_async_remote_copy(
            src_ref=src, dst_ref=dst, send_sem=send, recv_sem=recv,
            device_id={ctx_axis: to}, device_id_type=MESH,
        )

    def halo_copy(way, to):
        first = rows - HALO if way == 0 else 0
        return remote(
            h_hbm.at[pl.ds(first, HALO), :], prev if way == 0 else follow,
            halo_send.at[way], halo_recv.at[way], to,
        )

    def decay_copy():
        return remote(dec.at[other], pair_dec, d_send, d_recv, partner)

    def pair_copy(g):
        return remote(state.at[other, g], pair_state.at[g], p_send.at[g], p_recv.at[g], partner)

    def chain_copy(g):
        return remote(send_buf.at[g], chain_in.at[g], c_send.at[g], c_recv.at[g], target)

    def hand_copy(d, g):
        return remote(chain_in.at[g], carry.at[d, g], f_send.at[g], f_recv.at[g], partner)

    @pl.when(me < n_ctx - 1)
    def _():
        halo_copy(0, me + 1).start()

    @pl.when(me > 0)
    def _():
        halo_copy(1, me - 1).start()

    gain = gain_ref[...].reshape(1, width)
    blocks = width // GROUP
    turn = anti(GROUP)

    def turned(ref):
        return jnp.concatenate(
            [dot(ref[:, (blocks - 1 - j) * GROUP : (blocks - j) * GROUP], turn) for j in range(blocks)], axis=1
        )

    def scale(u):
        return lax.rsqrt(jnp.mean(u * u, axis=1, keepdims=True) + epsilon)

    h_copy.wait()
    here = h_buf[...].astype(f32)
    factor = scale(here)
    n_buf[HALO:ext, :] = (here * factor * gain).astype(bf16)
    n_buf[ext : ext + rows, :] = (turned(h_buf) * factor * gain).astype(bf16)

    @pl.when(me > 0)
    def _():
        halo_copy(0, me - 1).wait_recv()

    @pl.when(me == 0)
    def _():
        prev[...] = jnp.zeros_like(prev)

    @pl.when(me < n_ctx - 1)
    def _():
        halo_copy(1, me + 1).wait_recv()

    @pl.when(me == n_ctx - 1)
    def _():
        follow[...] = jnp.zeros_like(follow)

    prior = prev[...].astype(f32)
    n_buf[0:HALO, :] = (prior * scale(prior) * gain).astype(bf16)
    later = turned(follow)
    n_buf[ext + rows :, :] = (later * scale(later) * gain).astype(bf16)

    bc_copy.wait()
    bc_in = dot(n_buf[...], bcw[...]).astype(bf16).astype(f32)
    bc[0] = conv_fwd(bc_in[:ext], bck_ref[...], rows)
    bc[1] = conv_bwd(bc_in[ext:], bck_ref[...], rows)
    raw = lax.dot_general(
        n_buf[HALO : ext + rows, :], dtw_ref[...], (((1,), (1,)), ((), ())), preferred_element_type=f32
    ) + dtb_ref[...]
    step = jnp.maximum(raw, 0.0) + jnp.log1p(jnp.exp(-jnp.abs(raw)))
    heads = raw.shape[1]
    pad[...] = jnp.zeros_like(pad)
    pad[0, :, 0:heads] = step
    pad[1, :, 0:heads] = -step * jnp.exp(rate_ref[...])
    ahead_rows = iota((rows, rows), 0) - iota((rows, rows), 1)
    for d in range(2):
        part = slice(d * rows, (d + 1) * rows)
        mask = ahead_rows >= 0 if d == 0 else ahead_rows <= 0
        total = dot(mask.astype(f32), pad[1, part, :], highest)
        end = total[rows - 1 : rows] if d == 0 else total[0:1]
        delta[d] = pad[0, part, :]
        cum[d] = total
        cumt[d] = total.T
        wend[d] = jnp.exp(end - total) * pad[0, part, :]
        last = jnp.broadcast_to(jnp.exp(end), (8, LANES))
        for g in range(groups):
            dec[d, g] = dot(last, spread(g), highest)
    decay_copy().start()

    def x_unit(g, _):
        weight_copy(xw_hbm, xw, xw_sem, g).wait()
        x_in = dot(n_buf[...], xw[g]).astype(bf16).astype(f32)
        taps = xk_ref[:, pl.ds(pl.multiple_of(g * GROUP, GROUP), GROUP)]
        hot = spread(g)
        for d in range(2):
            x_conv = conv_fwd(x_in[:ext], taps, rows) if d == 0 else conv_bwd(x_in[ext:], taps, rows)
            x_buf[d, g] = x_conv
            weighted = (x_conv.astype(f32) * dot(wend[d], hot, highest)).astype(bf16)
            state[d, g] = lax.dot_general(
                bc[d, :, :STATE], weighted, (((0,), (0,)), ((), ())), preferred_element_type=f32
            ).astype(bf16)
        pair_copy(g).start()
        return 0

    lax.fori_loop(0, groups, x_unit, 0)

    for d in range(2):
        full = lax.dot_general(
            bc[d, :, STATE:], bc[d, :, :STATE], (((1,), (1,)), ((), ())), preferred_element_type=f32
        )
        gram[d] = jnp.where(ahead_rows >= 0 if d == 0 else ahead_rows <= 0, full, 0.0)

    def unit(g, _):
        weight_copy(zw_hbm, zw, zw_sem, g).wait()
        z_buf[g] = dot(n_buf[HALO : HALO + 2 * rows, :], zw[g]).astype(bf16)
        hot = spread(g)
        lane_head = iota((rows, GROUP), 1) // HEAD_DIM
        for d in range(2):
            scaled = x_buf[d, g].astype(f32) * dot(delta[d], hot, highest)
            cols = dot(cum[d], hot, highest)
            parts, values = [], []
            for j in range(GROUP // HEAD_DIM):
                column = cols[:, j * HEAD_DIM : j * HEAD_DIM + 1]
                row = cumt[d, pl.ds(g * (GROUP // HEAD_DIM) + j, 1), :]
                parts.append((jnp.exp(jnp.minimum(column - row, 0.0)) * gram[d]).astype(bf16))
                values.append(jnp.where(lane_head == j, scaled, 0.0).astype(bf16))
            y_buf[g, d] = dot(jnp.concatenate(parts, axis=1), jnp.concatenate(values, axis=0))
        return 0

    def chain(g, _):
        pair_copy(g).wait_recv()

        @pl.when(has_source)
        def _():
            chain_copy(g).wait_recv()

        @pl.when(jnp.logical_not(has_source))
        def _():
            chain_in[g] = jnp.zeros_like(chain_in[g])

        joined = chain_in[g].astype(f32) * pair_dec[g, 0:1, :] + pair_state[g].astype(f32)
        carry[mine, g] = joined.astype(bf16)

        @pl.when(has_target)
        def _():
            send_buf[g] = (joined * dec[mine, g, 0:1, :] + state[mine, g].astype(f32)).astype(bf16)
            chain_copy(g).start()

        @pl.when(has_source)
        def _():
            hand_copy(mine, g).start()

        return 0

    late = jnp.where(mine == 0, me // 2, n_ctx // 2 - 1 - me // 2)
    before = jnp.minimum(groups, late + jnp.where(late > 1, 1, 0))
    lax.fori_loop(0, before, unit, 0)
    decay_copy().wait_recv()
    lax.fori_loop(0, groups, chain, 0)
    lax.fori_loop(before, groups, unit, 0)

    out_gain = out_gain_ref[...].reshape(1, groups * GROUP)
    same = iota((GROUP, GROUP), 0) // HEAD_DIM == iota((GROUP, GROUP), 1) // HEAD_DIM
    average = jnp.where(same, 1.0 / HEAD_DIM, 0.0).astype(bf16)
    growth = [jnp.exp(cum[d]) for d in range(2)]
    for g in range(groups):
        hot = spread(g)

        @pl.when(other_source)
        def _():
            hand_copy(other, g).wait_recv()

        @pl.when(jnp.logical_not(other_source))
        def _():
            carry[other, g] = jnp.zeros_like(carry[other, g])

        for d in range(2):
            carried = dot(bc[d, :, STATE:], carry[d, g]) * dot(growth[d], hot, highest)
            value = (y_buf[g, d] + carried) * silu(z_buf[g, d * rows : (d + 1) * rows].astype(f32))
            square = value * value
            high = square.astype(bf16)
            low = (square - high.astype(f32)).astype(bf16)
            mean_sq = dot(high, average) + dot(low, average)
            lanes = slice(g * GROUP, (g + 1) * GROUP)
            gated[d, :, lanes] = (
                value * lax.rsqrt(mean_sq + epsilon) * out_gain[:, lanes]
            ).astype(bf16)

    o_copy.wait()
    flip = anti(LANES)
    blocks = ow_hbm.shape[1] // block

    def project(which):
        mine = pl.multiple_of(which * block, LANES)
        other = pl.multiple_of((blocks - 1 - which) * block, LANES)
        ahead = dot(gated[0], ow[:, pl.ds(mine, block)])
        back = dot(gated[1], ow[:, pl.ds(other, block)]).astype(bf16)
        count = block // LANES
        turned = [
            dot(back[:, (count - 1 - j) * LANES : (count - j) * LANES], flip) for j in range(count)
        ]
        return ahead + jnp.concatenate(turned, axis=1)

    def near(slot):
        return pltpu.make_async_remote_copy(
            src_ref=one_send.at[slot],
            dst_ref=one_recv.at[slot],
            send_sem=r_send.at[slot],
            recv_sem=r_recv.at[slot],
            device_id={head_axis: sibling},
            device_id_type=MESH,
        )

    far = pltpu.make_async_remote_copy(
        src_ref=two_send,
        dst_ref=two_recv,
        send_sem=r_send.at[2],
        recv_sem=r_recv.at[2],
        device_id={head_axis: across},
        device_id_type=MESH,
    )
    one_send[0] = project((1 - side) * 2 + (1 - core)).astype(bf16)
    near(0).start()
    partial = project(across)
    near(0).wait_recv()
    two_send[...] = (partial + one_recv[0].astype(f32)).astype(bf16)
    far.start()
    one_send[1] = project(sibling).astype(bf16)
    near(1).start()
    partial = project(place)
    residual = h_buf[:, pl.ds(pl.multiple_of(place * block, LANES), block)].astype(f32)
    near(1).wait_recv()
    partial = partial + one_recv[1].astype(f32)
    far.wait_recv()
    out_ref[...] = (residual + (partial + two_recv[...].astype(f32))).astype(out_ref.dtype)
    near(0).wait_send()
    near(1).wait_send()
    far.wait_send()


    @pl.when(me < n_ctx - 1)
    def _():
        halo_copy(0, me + 1).wait_send()

    @pl.when(me > 0)
    def _():
        halo_copy(1, me - 1).wait_send()

    decay_copy().wait_send()

    def drain(g, _):
        pair_copy(g).wait_send()

        @pl.when(has_target)
        def _():
            chain_copy(g).wait_send()

        @pl.when(has_source)
        def _():
            hand_copy(mine, g).wait_send()

        return 0

    lax.fori_loop(0, groups, drain, 0)


def per_device(
    mesh,
    hidden,
    norm_gain,
    x_weight,
    z_weight,
    bc_weight,
    dt_weight,
    x_kernel,
    bc_kernel,
    dt_bias,
    log_rate,
    out_gain,
    out_weight,
):
    rows, width = hidden.shape
    inner = x_weight.shape[1]
    groups = inner // GROUP
    block = width // mesh.shape["head"]
    ext = rows + HALO
    vmem = pl.BlockSpec(memory_space=pltpu.VMEM)
    hbm = pl.BlockSpec(memory_space=pl.ANY)
    dma = pltpu.SemaphoreType.DMA
    return pl.pallas_call(
        functools.partial(kernel, mesh.shape["ctx"], ("ctx", "head")),
        out_shape=jax.ShapeDtypeStruct((rows, block), hidden.dtype),
        in_specs=[vmem] * 7 + [hbm] * 5,
        out_specs=vmem,
        scratch_shapes=[
            pltpu.VMEM((rows, width), bf16),
            pltpu.VMEM((HALO, width), bf16),
            pltpu.VMEM((HALO, width), bf16),
            pltpu.VMEM((width, 2 * STATE), bf16),
            pltpu.VMEM((groups, width, GROUP), bf16),
            pltpu.VMEM((groups, width, GROUP), bf16),
            pltpu.VMEM((inner, width), bf16),
            pltpu.VMEM((2 * ext, width), bf16),
            pltpu.VMEM((2, 2 * rows, LANES), f32),
            pltpu.VMEM((2, rows, 2 * STATE), bf16),
            pltpu.VMEM((2, rows, LANES), f32),
            pltpu.VMEM((2, rows, LANES), f32),
            pltpu.VMEM((2, LANES, rows), f32),
            pltpu.VMEM((2, rows, LANES), f32),
            pltpu.VMEM((2, groups, 8, GROUP), f32),
            pltpu.VMEM((groups, 8, GROUP), f32),
            pltpu.VMEM((2, groups, rows, GROUP), bf16),
            pltpu.VMEM((groups, 2 * rows, GROUP), bf16),
            pltpu.VMEM((groups, 2, rows, GROUP), f32),
            pltpu.VMEM((2, rows, inner), bf16),
            pltpu.VMEM((2, rows, rows), f32),
            pltpu.VMEM((2, groups, STATE, GROUP), bf16),
            pltpu.VMEM((groups, STATE, GROUP), bf16),
            pltpu.VMEM((groups, STATE, GROUP), bf16),
            pltpu.VMEM((2, groups, STATE, GROUP), bf16),
            pltpu.VMEM((groups, STATE, GROUP), bf16),
            pltpu.VMEM((2, rows, block), bf16),
            pltpu.VMEM((2, rows, block), bf16),
            pltpu.VMEM((rows, block), bf16),
            pltpu.VMEM((rows, block), bf16),
            dma((3,)),
            dma((groups,)),
            dma((groups,)),
            dma((2,)),
            dma((2,)),
            dma,
            dma,
            dma((groups,)),
            dma((groups,)),
            dma((groups,)),
            dma((groups,)),
            dma((groups,)),
            dma((groups,)),
            dma((3,)),
            dma((3,)),
        ],
        compiler_params=pltpu.CompilerParams(
            collective_id=0, has_side_effects=True, vmem_limit_bytes=60 * 2**20
        ),
        cost_estimate=pl.CostEstimate(flops=12_000_000_000, bytes_accessed=24_000_000, transcendentals=5_000_000),
        name="mixer",
    )(
        norm_gain,
        dt_weight.T,
        x_kernel,
        bc_kernel,
        dt_bias[None],
        log_rate[None],
        out_gain,
        hidden,
        x_weight,
        z_weight,
        bc_weight,
        out_weight,
    )


def solution(mesh):
    return jax.shard_map(
        functools.partial(per_device, mesh),
        mesh=mesh,
        in_specs=(
            P("ctx", None),
            P(),
            P(None, "head"),
            P(None, "head"),
            P(),
            P(None, "head"),
            P(None, "head"),
            P(),
            P("head"),
            P("head"),
            P("head"),
            P("head", None),
        ),
        out_specs=P("ctx", "head"),
        check_vma=False,
    )
```

time: 108 us -> 67.8 us (0.63)
  Pallas kernels: 84 us -> 65.9 us
  local copies, waits for them, and re-layouts: 15.3 us -> 1.73 us
  starting transfers between devices: 6.17 us -> 0 us
  waiting for transfers between devices: 1.76 us -> 0 us
    pallas_call x2 -> x1, Pallas kernels: 84 us -> 65.9 us  [per_device(): pl.pallas_call(functools.partial(kernel, mesh.shape['ctx'], ('ctx', 'head...]
    unnamed x26 -> x1, local copies, waits for them, and re-layouts: 12.4 us -> 1.73 us
    ppermute x2 -> x0, starting transfers between devices: 6.17 us -> none  [the longest x1 4.88 us: per_device(): lax.ppermute(hidden[rows - HALO:], 'ctx', [(i, i + 1) for i in range(n_ct...]
    broadcast_in_dim x2 -> x0, local copies, waits for them, and re-layouts: 2.01 us -> none  [the longest x1 1.3 us: per_device(): out_gain[None]]
    ppermute x2 -> x0, waiting for transfers between devices: 1.76 us -> none  [the longest x1 1.76 us: per_device(): lax.ppermute(hidden[:HALO], 'ctx', [(i + 1, i) for i in range(n_ctx - 1)])]
  transfers between devices with their start and end apart: 2 -> 0, of which waited for: 1 -> 0; matrix products, arithmetic and copies ran while one was open for 3% -> 0% of each run, Pallas kernels for 0% -> 0%
where the time goes in v2:
time: 67.8 us; the launch traced here: 67.6 us
  Pallas kernels  65.9 us (97%)
  local copies, waits for them, and re-layouts  1.73 us (3%)
    pallas_call x1, Pallas kernels, per_device(): pl.pallas_call(functools.partial(kernel, mesh.shape['ctx'], ('ctx', 'head...  65.9 us
    unnamed x1, local copies, waits for them, and re-layouts  1.73 us

profile of v2, /device:TPU:0, one launch (start us, length us, event | category | flops | bytes accessed | tf_op | source)
XLA Modules:
  0.0 67.6 jit_solution(15910163737463507634)
XLA Ops:
  0.0 65.9 %mixer.1 = bf16[256,640]{1,0:T(8,128)(2,1)} custom-call(f32[2560]{0:T(1024)} %gain_ref.1, bf16[20,2560]{1,0:T(8,128)(2,1)} %bitcast.3, f32[4,1280]{1,0:T(4,128)} %xk_ref.1, f32[4,256]{1,0:T(4,128)} %bck_ref.1, f32[1,20]{1,0:T(1,128)} %bitcast.4, f32[1,20]{1,0:T(1,128)} %bitcast.5, f32[1280]{0:T(1024)} %out_gain_ref.1, bf16[256,2560]{1,0:T(8,128)(2,1)} %h_hbm.1, ...), custom_call_target="tpu_custom_call" | custom-call | flops 12000000000 | bytes 24000000 | tf_op jit(solution)/shard_map/mixer/pallas_call | solution.py:416
  65.9 1.7 %copy.14 = bf16[256,640]{1,0:T(8,128)(2,1)} copy(bf16[256,640]{1,0:T(8,128)(2,1)} %mixer.1) | data formatting | bytes 655360

commit v3 on v2

--- a/solution.py
+++ b/solution.py
@@ -28,16 +28,28 @@
 
 
 def silu(v):
-    return v / (1.0 + jnp.exp(-v))
+    half = 0.5 * v
+    return half + half * jnp.tanh(half)
+
+
+def pieces(v, count):
+    out = []
+    for _ in range(count):
+        part = v.astype(bf16)
+        out.append(part)
+        v = v - part.astype(f32)
+    return jnp.concatenate(out, axis=1)
 
 
 def anti(size):
     return (iota((size, size), 0) + iota((size, size), 1) == size - 1).astype(bf16)
 
 
-def spread(group):
-    head = group * (GROUP // HEAD_DIM) + iota((LANES, GROUP), 1) // HEAD_DIM
-    return (iota((LANES, GROUP), 0) == head).astype(f32)
+def spread(group, count=2, each=HEAD_DIM):
+    per = GROUP // HEAD_DIM
+    shape = (count * LANES, per * each)
+    head = group * per + iota(shape, 1) // each
+    return (lax.rem(iota(shape, 0), LANES) == head).astype(bf16)
 
 
 def conv_fwd(ext, taps, rows):
@@ -58,7 +70,7 @@
     n_ctx, axes,
     gain_ref, dtw_ref, xk_ref, bck_ref, dtb_ref, rate_ref, out_gain_ref, h_hbm, xw_hbm, zw_hbm, bcw_hbm, ow_hbm,
     out_ref,
-    h_buf, prev, follow, bcw, xw, zw, ow, n_buf, pad, bc, delta, cum, cumt, wend, dec, pair_dec,
+    h_buf, prev, follow, bcw, xw, zw, ow, n_buf, pad, bc, delta, cum, cumt, wend, growth, mid, dec, pair_dec, x_in, out_gain,
     x_buf, z_buf, y_buf, gated, gram, state, pair_state, chain_in, carry, send_buf,
     one_send, one_recv, two_send, two_recv,
     in_sem, xw_sem, zw_sem, halo_send, halo_recv, d_send, d_recv, p_send, p_recv, c_send, c_recv, f_send, f_recv,
@@ -71,6 +83,7 @@
     groups = x_buf.shape[1]
     block = out_ref.shape[1]
     ext = rows + HALO
+    half = rows // 2
     core = lax.rem(place, 2)
     side = place // 2
     sibling = side * 2 + (1 - core)
@@ -204,31 +217,43 @@
         mask = ahead_rows >= 0 if d == 0 else ahead_rows <= 0
         total = dot(mask.astype(f32), pad[1, part, :], highest)
         end = total[rows - 1 : rows] if d == 0 else total[0:1]
-        delta[d] = pad[0, part, :]
-        cum[d] = total
         cumt[d] = total.T
-        wend[d] = jnp.exp(end - total) * pad[0, part, :]
-        last = jnp.broadcast_to(jnp.exp(end), (8, LANES))
+        step_d = pad[0, part, :]
+        delta[d] = pieces(step_d, 2)
+        cum[d] = pieces(total, 3)
+        wend[d] = pieces(jnp.exp(end - total) * step_d, 2)
+        growth[d] = pieces(jnp.exp(total), 2)
+        edge = total[half - 1 : half] if d == 0 else total[half : half + 1]
+        low_part, high_part = total[:half], total[half:]
+        if d == 0:
+            mids = [jnp.exp(edge - low_part) * step_d[:half], jnp.exp(high_part - edge)]
+        else:
+            mids = [jnp.exp(low_part - edge), jnp.exp(edge - high_part) * step_d[half:]]
+        mid[d] = pieces(jnp.concatenate(mids, axis=0), 2)
+        last = pieces(jnp.broadcast_to(jnp.exp(end), (8, LANES)), 3)
         for g in range(groups):
-            dec[d, g] = dot(last, spread(g), highest)
+            dec[d, g] = dot(last, spread(g, 3))
     decay_copy().start()
 
-    def x_unit(g, _):
+    def x_project(g):
         weight_copy(xw_hbm, xw, xw_sem, g).wait()
-        x_in = dot(n_buf[...], xw[g]).astype(bf16).astype(f32)
-        taps = xk_ref[:, pl.ds(pl.multiple_of(g * GROUP, GROUP), GROUP)]
+        x_in[g % 2] = dot(n_buf[...], xw[g]).astype(bf16)
+
+    x_project(0)
+    for g in range(groups):
+        if g + 1 < groups:
+            x_project(g + 1)
+        now = x_in[g % 2].astype(f32)
+        taps = xk_ref[:, g * GROUP : (g + 1) * GROUP]
         hot = spread(g)
         for d in range(2):
-            x_conv = conv_fwd(x_in[:ext], taps, rows) if d == 0 else conv_bwd(x_in[ext:], taps, rows)
+            x_conv = conv_fwd(now[:ext], taps, rows) if d == 0 else conv_bwd(now[ext:], taps, rows)
             x_buf[d, g] = x_conv
-            weighted = (x_conv.astype(f32) * dot(wend[d], hot, highest)).astype(bf16)
+            weighted = (x_conv.astype(f32) * dot(wend[d], hot)).astype(bf16)
             state[d, g] = lax.dot_general(
                 bc[d, :, :STATE], weighted, (((0,), (0,)), ((), ())), preferred_element_type=f32
             ).astype(bf16)
         pair_copy(g).start()
-        return 0
-
-    lax.fori_loop(0, groups, x_unit, 0)
 
     for d in range(2):
         full = lax.dot_general(
@@ -238,19 +263,32 @@
 
     def unit(g, _):
         weight_copy(zw_hbm, zw, zw_sem, g).wait()
-        z_buf[g] = dot(n_buf[HALO : HALO + 2 * rows, :], zw[g]).astype(bf16)
+        z_in = dot(n_buf[HALO : HALO + 2 * rows, :], zw[g]).astype(bf16)
+        z_buf[g, 0] = z_in[:rows]
+        z_buf[g, 1] = z_in[rows:]
         hot = spread(g)
-        lane_head = iota((rows, GROUP), 1) // HEAD_DIM
+        wide = spread(g, 3, half)
+        per = GROUP // HEAD_DIM
+        lane_head = iota((half, GROUP), 1) // HEAD_DIM
         for d in range(2):
-            scaled = x_buf[d, g].astype(f32) * dot(delta[d], hot, highest)
-            cols = dot(cum[d], hot, highest)
-            parts, values = [], []
-            for j in range(GROUP // HEAD_DIM):
-                column = cols[:, j * HEAD_DIM : j * HEAD_DIM + 1]
-                row = cumt[d, pl.ds(g * (GROUP // HEAD_DIM) + j, 1), :]
-                parts.append((jnp.exp(jnp.minimum(column - row, 0.0)) * gram[d]).astype(bf16))
-                values.append(jnp.where(lane_head == j, scaled, 0.0).astype(bf16))
-            y_buf[g, d] = dot(jnp.concatenate(parts, axis=1), jnp.concatenate(values, axis=0))
+            x_here = x_buf[d, g].astype(f32)
+            scaled = x_here * dot(delta[d], hot)
+            cols = dot(cum[d], wide)
+            middle = dot(mid[d], hot)
+            for b in range(2):
+                here = slice(b * half, (b + 1) * half)
+                there = slice((1 - b) * half, (2 - b) * half)
+                parts, values = [], []
+                for j in range(per):
+                    column = cols[here, j * half : (j + 1) * half]
+                    row = cumt[d, pl.ds(g * per + j, 1), :][:, here]
+                    parts.append((jnp.exp(jnp.minimum(column - row, 0.0)) * gram[d, here, here]).astype(bf16))
+                    values.append(jnp.where(lane_head == j, scaled[here], 0.0).astype(bf16))
+                y = dot(jnp.concatenate(parts, axis=1), jnp.concatenate(values, axis=0))
+                if b != d:
+                    sent = (x_here[there] * middle[there]).astype(bf16)
+                    y = y + middle[here] * dot(gram[d, here, there].astype(bf16), sent)
+                y_buf[g, d, here] = y
         return 0
 
     def chain(g, _):
@@ -285,13 +323,25 @@
     lax.fori_loop(0, groups, chain, 0)
     lax.fori_loop(before, groups, unit, 0)
 
-    out_gain = out_gain_ref[...].reshape(1, groups * GROUP)
     same = iota((GROUP, GROUP), 0) // HEAD_DIM == iota((GROUP, GROUP), 1) // HEAD_DIM
     average = jnp.where(same, 1.0 / HEAD_DIM, 0.0).astype(bf16)
-    growth = [jnp.exp(cum[d]) for d in range(2)]
-    for g in range(groups):
-        hot = spread(g)
-
+    out_gain[...] = out_gain_ref[...].reshape(1, groups * GROUP)
+
+    def finish(d, g):
+        carried = dot(bc[d, :, STATE:], carry[d, g]) * dot(growth[d], spread(g))
+        value = (y_buf[g, d] + carried) * silu(z_buf[g, d].astype(f32))
+        square = value * value
+        high = square.astype(bf16)
+        low = (square - high.astype(f32)).astype(bf16)
+        mean_sq = dot(high, average) + dot(low, average)
+        lanes = pl.ds(pl.multiple_of(g * GROUP, GROUP), GROUP)
+        gated[d, :, lanes] = (value * lax.rsqrt(mean_sq + epsilon) * out_gain[:, lanes]).astype(bf16)
+
+    def finish_mine(g, _):
+        finish(mine, g)
+        return 0
+
+    def finish_other(g, _):
         @pl.when(other_source)
         def _():
             hand_copy(other, g).wait_recv()
@@ -300,17 +350,11 @@
         def _():
             carry[other, g] = jnp.zeros_like(carry[other, g])
 
-        for d in range(2):
-            carried = dot(bc[d, :, STATE:], carry[d, g]) * dot(growth[d], hot, highest)
-            value = (y_buf[g, d] + carried) * silu(z_buf[g, d * rows : (d + 1) * rows].astype(f32))
-            square = value * value
-            high = square.astype(bf16)
-            low = (square - high.astype(f32)).astype(bf16)
-            mean_sq = dot(high, average) + dot(low, average)
-            lanes = slice(g * GROUP, (g + 1) * GROUP)
-            gated[d, :, lanes] = (
-                value * lax.rsqrt(mean_sq + epsilon) * out_gain[:, lanes]
-            ).astype(bf16)
+        finish(other, g)
+        return 0
+
+    lax.fori_loop(0, groups, finish_mine, 0)
+    lax.fori_loop(0, groups, finish_other, 0)
 
     o_copy.wait()
     flip = anti(LANES)
@@ -429,14 +473,18 @@
             pltpu.VMEM((2 * ext, width), bf16),
             pltpu.VMEM((2, 2 * rows, LANES), f32),
             pltpu.VMEM((2, rows, 2 * STATE), bf16),
-            pltpu.VMEM((2, rows, LANES), f32),
-            pltpu.VMEM((2, rows, LANES), f32),
+            pltpu.VMEM((2, rows, 2 * LANES), bf16),
+            pltpu.VMEM((2, rows, 3 * LANES), bf16),
             pltpu.VMEM((2, LANES, rows), f32),
-            pltpu.VMEM((2, rows, LANES), f32),
+            pltpu.VMEM((2, rows, 2 * LANES), bf16),
+            pltpu.VMEM((2, rows, 2 * LANES), bf16),
+            pltpu.VMEM((2, rows, 2 * LANES), bf16),
             pltpu.VMEM((2, groups, 8, GROUP), f32),
             pltpu.VMEM((groups, 8, GROUP), f32),
+            pltpu.VMEM((2, 2 * ext, GROUP), bf16),
+            pltpu.VMEM((1, inner), f32),
             pltpu.VMEM((2, groups, rows, GROUP), bf16),
-            pltpu.VMEM((groups, 2 * rows, GROUP), bf16),
+            pltpu.VMEM((groups, 2, rows, GROUP), bf16),
             pltpu.VMEM((groups, 2, rows, GROUP), f32),
             pltpu.VMEM((2, rows, inner), bf16),
             pltpu.VMEM((2, rows, rows), f32),

time: 67.8 us -> 61.9 us (0.913)
  Pallas kernels: 65.9 us -> 60 us
    pallas_call x1, Pallas kernels: 65.9 us -> 60 us  [per_device(): pl.pallas_call(functools.partial(kernel, mesh.shape['ctx'], ('ctx', 'head...]
where the time goes in v3:
time: 61.9 us; the launch traced here: 61.8 us
  Pallas kernels  60 us (97%)
  local copies, waits for them, and re-layouts  1.73 us (3%)
    pallas_call x1, Pallas kernels, per_device(): pl.pallas_call(functools.partial(kernel, mesh.shape['ctx'], ('ctx', 'head...  60 us
    unnamed x1, local copies, waits for them, and re-layouts  1.73 us

profile of v3, /device:TPU:0, one launch (start us, length us, event | category | flops | bytes accessed | tf_op | source)
XLA Modules:
  0.0 61.8 jit_solution(2133813556743899432)
XLA Ops:
  0.0 60.0 %mixer.1 = bf16[256,640]{1,0:T(8,128)(2,1)} custom-call(f32[2560]{0:T(1024)} %gain_ref.1, bf16[20,2560]{1,0:T(8,128)(2,1)} %bitcast.3, f32[4,1280]{1,0:T(4,128)} %xk_ref.1, f32[4,256]{1,0:T(4,128)} %bck_ref.1, f32[1,20]{1,0:T(1,128)} %bitcast.4, f32[1,20]{1,0:T(1,128)} %bitcast.5, f32[1280]{0:T(1024)} %out_gain_ref.1, bf16[256,2560]{1,0:T(8,128)(2,1)} %h_hbm.1, ...), custom_call_target="tpu_custom_call" | custom-call | flops 12000000000 | bytes 24000000 | tf_op jit(solution)/shard_map/mixer/pallas_call | solution.py:460
  60.0 1.7 %copy.14 = bf16[256,640]{1,0:T(8,128)(2,1)} copy(bf16[256,640]{1,0:T(8,128)(2,1)} %mixer.1) | data formatting | bytes 655360

commit v4 on v3

--- a/solution.py
+++ b/solution.py
@@ -317,7 +317,7 @@
         return 0
 
     late = jnp.where(mine == 0, me // 2, n_ctx // 2 - 1 - me // 2)
-    before = jnp.minimum(groups, late + jnp.where(late > 1, 1, 0))
+    before = jnp.minimum(groups, 2 * late)
     lax.fori_loop(0, before, unit, 0)
     decay_copy().wait_recv()
     lax.fori_loop(0, groups, chain, 0)
@@ -360,53 +360,61 @@
     flip = anti(LANES)
     blocks = ow_hbm.shape[1] // block
 
-    def project(which):
-        mine = pl.multiple_of(which * block, LANES)
-        other = pl.multiple_of((blocks - 1 - which) * block, LANES)
-        ahead = dot(gated[0], ow[:, pl.ds(mine, block)])
-        back = dot(gated[1], ow[:, pl.ds(other, block)]).astype(bf16)
-        count = block // LANES
+    cuts = ((0, GROUP), (GROUP, block))
+
+    def project(which, first, last):
+        here = pl.multiple_of(which * block + first, LANES)
+        there = pl.multiple_of((blocks - which) * block - last, LANES)
+        ahead = dot(gated[0], ow[:, pl.ds(here, last - first)])
+        back = dot(gated[1], ow[:, pl.ds(there, last - first)]).astype(bf16)
+        count = (last - first) // LANES
         turned = [
             dot(back[:, (count - 1 - j) * LANES : (count - j) * LANES], flip) for j in range(count)
         ]
         return ahead + jnp.concatenate(turned, axis=1)
 
-    def near(slot):
+    def reduce_copy(src, dst, slot, cut, peer):
+        lanes = pl.ds(cut[0], cut[1] - cut[0])
         return pltpu.make_async_remote_copy(
-            src_ref=one_send.at[slot],
-            dst_ref=one_recv.at[slot],
+            src_ref=src.at[:, lanes],
+            dst_ref=dst.at[:, lanes],
             send_sem=r_send.at[slot],
             recv_sem=r_recv.at[slot],
-            device_id={head_axis: sibling},
+            device_id={head_axis: peer},
             device_id_type=MESH,
         )
 
-    far = pltpu.make_async_remote_copy(
-        src_ref=two_send,
-        dst_ref=two_recv,
-        send_sem=r_send.at[2],
-        recv_sem=r_recv.at[2],
-        device_id={head_axis: across},
-        device_id_type=MESH,
-    )
-    one_send[0] = project((1 - side) * 2 + (1 - core)).astype(bf16)
-    near(0).start()
-    partial = project(across)
-    near(0).wait_recv()
-    two_send[...] = (partial + one_recv[0].astype(f32)).astype(bf16)
-    far.start()
-    one_send[1] = project(sibling).astype(bf16)
-    near(1).start()
-    partial = project(place)
+    nears = [reduce_copy(one_send.at[0], one_recv.at[0], i, cut, sibling) for i, cut in enumerate(cuts)]
+    fars = [reduce_copy(two_send, two_recv, 2 + i, cut, across) for i, cut in enumerate(cuts)]
+    last_near = reduce_copy(one_send.at[1], one_recv.at[1], 4, (0, block), sibling)
+    opposite = (1 - side) * 2 + (1 - core)
+
+    def pass_on(i, partial):
+        lanes = slice(*cuts[i])
+        nears[i].wait_recv()
+        two_send[:, lanes] = (partial + one_recv[0, :, lanes].astype(f32)).astype(bf16)
+        fars[i].start()
+
+    for i, cut in enumerate(cuts):
+        one_send[0, :, cut[0] : cut[1]] = project(opposite, *cut).astype(bf16)
+        nears[i].start()
+        if i > 0:
+            pass_on(i - 1, partial)
+        partial = project(across, *cut)
+    pass_on(len(cuts) - 1, partial)
+    one_send[1] = project(sibling, 0, block).astype(bf16)
+    last_near.start()
+    partial = project(place, 0, block)
     residual = h_buf[:, pl.ds(pl.multiple_of(place * block, LANES), block)].astype(f32)
-    near(1).wait_recv()
+    last_near.wait_recv()
     partial = partial + one_recv[1].astype(f32)
-    far.wait_recv()
-    out_ref[...] = (residual + (partial + two_recv[...].astype(f32))).astype(out_ref.dtype)
-    near(0).wait_send()
-    near(1).wait_send()
-    far.wait_send()
-
+    for i, cut in enumerate(cuts):
+        lanes = slice(*cut)
+        fars[i].wait_recv()
+        summed = partial[:, lanes] + two_recv[:, lanes].astype(f32)
+        out_ref[:, lanes] = (residual[:, lanes] + summed).astype(out_ref.dtype)
+    for copy in (*nears, *fars, last_near):
+        copy.wait_send()
 
     @pl.when(me < n_ctx - 1)
     def _():
@@ -510,8 +518,8 @@
             dma((groups,)),
             dma((groups,)),
             dma((groups,)),
-            dma((3,)),
-            dma((3,)),
+            dma((5,)),
+            dma((5,)),
         ],
         compiler_params=pltpu.CompilerParams(
             collective_id=0, has_side_effects=True, vmem_limit_bytes=60 * 2**20

time: 61.9 us -> 59.5 us (0.961)
  Pallas kernels: 60 us -> 57.6 us
    pallas_call x1, Pallas kernels: 60 us -> 57.6 us  [per_device(): pl.pallas_call(functools.partial(kernel, mesh.shape['ctx'], ('ctx', 'head...]
where the time goes in v4:
time: 59.5 us; the launch traced here: 59.4 us
  Pallas kernels  57.6 us (97%)
  local copies, waits for them, and re-layouts  1.73 us (3%)
    pallas_call x1, Pallas kernels, per_device(): pl.pallas_call(functools.partial(kernel, mesh.shape['ctx'], ('ctx', 'head...  57.6 us
    unnamed x1, local copies, waits for them, and re-layouts  1.73 us

profile of v4, /device:TPU:0, one launch (start us, length us, event | category | flops | bytes accessed | tf_op | source)
XLA Modules:
  0.0 59.4 jit_solution(4403633096077826294)
XLA Ops:
  0.0 57.6 %mixer.1 = bf16[256,640]{1,0:T(8,128)(2,1)} custom-call(f32[2560]{0:T(1024)} %gain_ref.1, bf16[20,2560]{1,0:T(8,128)(2,1)} %bitcast.3, f32[4,1280]{1,0:T(4,128)} %xk_ref.1, f32[4,256]{1,0:T(4,128)} %bck_ref.1, f32[1,20]{1,0:T(1,128)} %bitcast.4, f32[1,20]{1,0:T(1,128)} %bitcast.5, f32[1280]{0:T(1024)} %out_gain_ref.1, bf16[256,2560]{1,0:T(8,128)(2,1)} %h_hbm.1, ...), custom_call_target="tpu_custom_call" | custom-call | flops 12000000000 | bytes 24000000 | tf_op jit(solution)/shard_map/mixer/pallas_call | solution.py:468
  57.6 1.7 %copy.14 = bf16[256,640]{1,0:T(8,128)(2,1)} copy(bf16[256,640]{1,0:T(8,128)(2,1)} %mixer.1) | data formatting | bytes 655360

commit v5 on v4

--- a/solution.py
+++ b/solution.py
@@ -318,11 +318,6 @@
 
     late = jnp.where(mine == 0, me // 2, n_ctx // 2 - 1 - me // 2)
     before = jnp.minimum(groups, 2 * late)
-    lax.fori_loop(0, before, unit, 0)
-    decay_copy().wait_recv()
-    lax.fori_loop(0, groups, chain, 0)
-    lax.fori_loop(before, groups, unit, 0)
-
     same = iota((GROUP, GROUP), 0) // HEAD_DIM == iota((GROUP, GROUP), 1) // HEAD_DIM
     average = jnp.where(same, 1.0 / HEAD_DIM, 0.0).astype(bf16)
     out_gain[...] = out_gain_ref[...].reshape(1, groups * GROUP)
@@ -353,8 +348,28 @@
         finish(other, g)
         return 0
 
-    lax.fori_loop(0, groups, finish_mine, 0)
-    lax.fori_loop(0, groups, finish_other, 0)
+    done = before >= groups
+    early = jnp.logical_and(done, jnp.logical_not(other_source))
+
+    def link(g, _):
+        chain(g, 0)
+
+        @pl.when(done)
+        def _():
+            finish(mine, g)
+
+        @pl.when(early)
+        def _():
+            finish_other(g, 0)
+
+        return 0
+
+    lax.fori_loop(0, before, unit, 0)
+    decay_copy().wait_recv()
+    lax.fori_loop(0, groups, link, 0)
+    lax.fori_loop(before, groups, unit, 0)
+    lax.fori_loop(0, jnp.where(done, 0, groups), finish_mine, 0)
+    lax.fori_loop(0, jnp.where(early, 0, groups), finish_other, 0)
 
     o_copy.wait()
     flip = anti(LANES)

time: 59.5 us -> 57.4 us (0.965); the launches traced: 59.4 us -> 56.4 us
  Pallas kernels: 57.6 us -> 54.7 us
    pallas_call x1, Pallas kernels: 57.6 us -> 54.7 us  [per_device(): pl.pallas_call(functools.partial(kernel, mesh.shape['ctx'], ('ctx', 'head...]
where the time goes in v5:
time: 57.4 us; the launch traced here: 56.4 us
  Pallas kernels  54.7 us (95%)
  local copies, waits for them, and re-layouts  1.73 us (3%)
    pallas_call x1, Pallas kernels, per_device(): pl.pallas_call(functools.partial(kernel, mesh.shape['ctx'], ('ctx', 'head...  54.7 us
    unnamed x1, local copies, waits for them, and re-layouts  1.73 us

profile of v5, /device:TPU:0, one launch (start us, length us, event | category | flops | bytes accessed | tf_op | source)
XLA Modules:
  0.0 56.4 jit_solution(15704565458184795219)
XLA Ops:
  0.0 54.7 %mixer.1 = bf16[256,640]{1,0:T(8,128)(2,1)} custom-call(f32[2560]{0:T(1024)} %gain_ref.1, bf16[20,2560]{1,0:T(8,128)(2,1)} %bitcast.3, f32[4,1280]{1,0:T(4,128)} %xk_ref.1, f32[4,256]{1,0:T(4,128)} %bck_ref.1, f32[1,20]{1,0:T(1,128)} %bitcast.4, f32[1,20]{1,0:T(1,128)} %bitcast.5, f32[1280]{0:T(1024)} %out_gain_ref.1, bf16[256,2560]{1,0:T(8,128)(2,1)} %h_hbm.1, ...), custom_call_target="tpu_custom_call" | custom-call | flops 12000000000 | bytes 24000000 | tf_op jit(solution)/shard_map/mixer/pallas_call | solution.py:483
  54.7 1.7 %copy.14 = bf16[256,640]{1,0:T(8,128)(2,1)} copy(bf16[256,640]{1,0:T(8,128)(2,1)} %mixer.1) | data formatting | bytes 655360
